TPU v7x, 128 devices: a whole 4x4x4 slice. The times are simulated.
128 devices in a mesh: gx: 8 (over x_lo, y), gy: 16 (over x_hi, z, core).
Axes of the slice: x: 4 (x_hi: 2, x_lo: 2; x = x_hi * 2 + x_lo), y: 4, z: 4, core: 2. Of those that a mesh axis runs over, the one named last changes fastest.
Arguments:
- coefficients: bfloat16 [16, 8, 256, 2048], P('gy', 'gx'), may hold values from -6 to 6
- src_blocks: bfloat16 [4, 16, 2, 2, 32, 32], replicated, may hold values from -0.5 to 0.5
- mid_blocks: bfloat16 [16, 2, 32, 32], replicated, may hold values from -0.75 to 0.75
- obs_blocks: bfloat16 [4, 16, 2, 2, 32, 32], replicated, may hold values from -0.5 to 0.5
- block_ids: int32 [16, 8, 256, 9], P('gy', 'gx'), may hold values from 0 to 15
- partner_perm: int32 [8, 256], replicated, may hold values from 0 to 255, each once within a row
- owner_order: int32 [16, 8, 256], P('gy', 'gx'), may hold values from 0 to 255, each once within a row
Outputs:
- field_coeffs: bfloat16 [16, 8, 256, 2048], P('gy', 'gx')
Inputs may be any that keep to these rules, and one draw needn't show every extreme that they name: `partner_perm`: each row is a permutation. `owner_order`: each device's row is a permutation.
All inputs are finite; a program needn't handle non-finite values.
Results may differ from a plain program's by a relative error of at most 0.019.
Values may be sent and summed in bfloat16 or wider, within the bound.
No kernel may reach another device: no remote copies, remote signals or barrier semaphores. Data moves between devices by JAX's collectives and lax.ppermute only.
A program may use at most 64 MiB of HBM per device.

v0:
```python
import functools

import jax
import jax.numpy as jnp
import numpy as np
from jax import lax
from jax.experimental import pallas as pl
from jax.experimental.pallas import tpu as pltpu
from jax.sharding import PartitionSpec as P

NA = 8
MEMBERS = 16
CLUSTERS = 256
LANES = 128
HALF = 64
IDS = 16
EXTRA = 2 * IDS
AXES = ("gx", "gy")
BF = jnp.bfloat16
F32 = jnp.float32


def number(a, b, c):
    return 16 * a + 2 * b + c


SRC_GROUPS = [[number((t // 2) ^ b, b, t % 2) for t in range(MEMBERS)] for b in range(NA)]
MID_GROUPS = [[number(a, r ^ a, c) for a in range(NA)] for r in range(NA) for c in range(2)]
OBS_GROUPS = [[number(a, (t // 2) ^ a, t % 2) for t in range(MEMBERS)] for a in range(NA)]


def position_order():
    row = np.arange(CLUSTERS)
    b, q, r, c = row >> 5, (row >> 4) & 1, (row >> 1) & 7, row & 1
    return ((r ^ b) * 16 + b * 2 + c) * 2 + q


ORDER = position_order()


def pack_kernel(coef_ref, ids_ref, send_ref, ordered_ref, out_ref):
    ids = jnp.concatenate([ids_ref[...].astype(F32), jnp.zeros((CLUSTERS, LANES - 9), F32)], axis=1).T[:MEMBERS]
    ordered = jnp.dot(ids.astype(BF), ordered_ref[...], preferred_element_type=F32)
    pad = jnp.zeros((3, CLUSTERS), F32)
    source = jnp.concatenate([ids[:4], send_ref[...].astype(F32), pad], axis=0)
    other = jnp.concatenate([ordered[4:8], ids[8:9], pad], axis=0)
    extra = jnp.concatenate([source[:, :LANES], source[:, LANES:], other[:, :LANES], other[:, LANES:]], axis=0)
    extra = extra.astype(BF)
    for t in range(MEMBERS):
        out_ref[t, :CLUSTERS, :] = coef_ref[:, t * LANES : (t + 1) * LANES]
        out_ref[t, CLUSTERS:, :] = extra


def turned_weights(block, parts):
    rows = []
    for low in range(4):
        each = [(4 * high + low, part) for high in range(4) for part in range(parts)]
        top = [(block(k, p, 0), -block(k, p, 1)) for k, p in each]
        bottom = [(block(k, p, 1), block(k, p, 0)) for k, p in each]
        rows += [jnp.concatenate([piece for pair in half for piece in pair], axis=1) for half in (top, bottom)]
    return jnp.concatenate(rows, axis=0).T.astype(BF)


def table_kernel(
    src_ref, mid_ref, obs_ref, perm_ref, ordered_ref, order_ref,
    src_perm_ref, obs_perm_ref, src_w_ref, obs_w_ref, mid_w_ref,
):
    perm = perm_ref[...].astype(F32)
    moved = jnp.dot(perm.astype(BF), ordered_ref[...], preferred_element_type=F32)
    turned = jnp.concatenate([perm, moved, jnp.zeros((LANES - 16, CLUSTERS), F32)], axis=0).T
    shape = (CLUSTERS, CLUSTERS)
    count = lax.broadcasted_iota(jnp.int32, shape, 1).astype(F32)
    order = jnp.broadcast_to(order_ref[...], shape)

    def match(column, against):
        return jnp.where(jnp.broadcast_to(column, shape) == against, 1.0, 0.0).astype(BF)

    for l in range(4):
        src_perm_ref[l] = match(turned[:, l : l + 1], count)
        at = 12 + l if l < 3 else 7
        obs_perm_ref[l] = match(turned[:, at : at + 1], order)
    obs_perm_ref[4] = match(lax.broadcasted_iota(jnp.int32, shape, 0).astype(F32), order)

    def weights(l, carry):
        src_w_ref[l] = turned_weights(lambda k, p, i: src_ref[l, k, p, i].astype(F32), 2)
        obs_w_ref[l] = turned_weights(lambda k, p, i: obs_ref[l, k, p, i].astype(F32), 2)
        return carry

    lax.fori_loop(0, 4, weights, 0)
    mid_w_ref[...] = turned_weights(lambda k, p, i: mid_ref[k, i].astype(F32), 1)


def spread_kinds(kt_ref, kb_ref, row):
    for m in range(MEMBERS):
        for half in range(2):
            col = m * IDS + 8 * half + row
            kinds = jnp.broadcast_to(kt_ref[:, col : col + 1], (LANES, LANES))
            high = jnp.floor(kinds * 0.25)
            at = slice(half * LANES, (half + 1) * LANES)
            kb_ref[0, m, at, :] = high.astype(BF)
            kb_ref[1, m, at, :] = (kinds - 4.0 * high).astype(BF)


def swap_halves(x):
    return jnp.concatenate([x[:, HALF:], x[:, :HALF]], axis=1)


def low_lanes():
    return lax.broadcasted_iota(jnp.int32, (CLUSTERS, LANES), 1) < HALF


def choose(prod_u, prod_v, low):
    second = low >= 2.0
    odd = (low == 1.0) | (low == 3.0)
    fu = jnp.where(second, prod_u[:, LANES:].astype(BF), prod_u[:, :LANES].astype(BF))
    fv = jnp.where(second, prod_v[:, LANES:].astype(BF), prod_v[:, :LANES].astype(BF))
    left = jnp.where(odd, swap_halves(fu), fu)
    right = jnp.where(odd, fv, swap_halves(fv))
    return jnp.concatenate([left[:, :HALF], right[:, HALF:]], axis=1)


def expand(x, high):
    zero = jnp.zeros_like(x)
    return jnp.concatenate([jnp.where(high == float(j), x, zero) for j in range(4)], axis=1)


def level(read, write, perm, weights, kb_ref, mask, own_perm=None):
    def body(i, carry):
        ms = [2 * i, 2 * i + 1]
        far = jnp.concatenate([read(m ^ mask) for m in ms], axis=1)
        far = jnp.dot(perm, far, preferred_element_type=F32).astype(BF)
        own = jnp.concatenate([read(m) for m in ms], axis=1)
        if own_perm is not None:
            own = jnp.dot(own_perm, own, preferred_element_type=F32).astype(BF)
        rows = []
        for k, m in enumerate(ms):
            x = own[:, k * LANES : (k + 1) * LANES]
            y = far[:, k * LANES : (k + 1) * LANES]
            high = kb_ref[0, m]
            rows.append(expand(jnp.concatenate([x[:, :HALF], y[:, :HALF]], axis=1), high))
            rows.append(expand(jnp.concatenate([x[:, HALF:], y[:, HALF:]], axis=1), high))
        prod = jnp.dot(jnp.concatenate(rows, axis=0), weights[...], preferred_element_type=F32)
        for k, m in enumerate(ms):
            at = 2 * k * CLUSTERS
            write(m, choose(prod[at : at + CLUSTERS], prod[at + CLUSTERS : at + 2 * CLUSTERS], kb_ref[1, m]))
        return carry

    lax.fori_loop(0, MEMBERS // 2, body, 0)


def source_kernel(place_ref, x_ref, perm_ref, w_ref, out_ref, kt_ref, kb_ref, s_ref, f_ref):
    b = place_ref[0]
    kt_ref[...] = x_ref[:, CLUSTERS : CLUSTERS + IDS, :].reshape(MEMBERS * IDS, LANES).astype(F32).T
    for l, mask in enumerate((2, 4, 8, 1)):
        spread_kinds(kt_ref, kb_ref, l)

        def read(m, l=l):
            return x_ref[m, :CLUSTERS, :] if l == 0 else s_ref[(l - 1) % 2, m]

        def write(m, value, l=l):
            s_ref[l % 2, m] = value

        level(read, write, perm_ref[l], w_ref.at[l], kb_ref, mask)
    lane = lax.broadcasted_iota(jnp.int32, (LANES, LANES), 1).astype(F32)
    for m in range(MEMBERS):
        picks = []
        for half in range(2):
            col = m * IDS + 8 * half + 4
            at = jnp.broadcast_to(kt_ref[:, col : col + 1], (LANES, LANES))
            picks.append(
                jnp.concatenate([(at == lane).astype(F32), (at == lane + LANES).astype(F32)], axis=1).astype(BF)
            )
        sent = jnp.dot(jnp.concatenate(picks, axis=0), s_ref[1, m], preferred_element_type=F32)
        f_ref[m * CLUSTERS : (m + 1) * CLUSTERS, :] = sent
    for h in range(NA):
        for n in range(MEMBERS):
            slot = (h * MEMBERS + (n ^ (2 * h))) * 2
            parts = [
                f_ref[pl.ds(m0 * CLUSTERS + slot + q, 8, stride=CLUSTERS), :] for q in range(2) for m0 in (0, 8)
            ]
            out_ref[h, n * EXTRA : (n + 1) * EXTRA, :] = jnp.concatenate(parts, axis=0).astype(BF)
        for c in range(2):
            at = MEMBERS * EXTRA + c * IDS
            out_ref[h, at : at + IDS, :] = x_ref[(h ^ b) * 2 + c, CLUSTERS + IDS :, :]


def observation_kernel(place_ref, r_ref, perm_ref, w_ref, wmid_ref, out_ref, kt_ref, kb_ref, s_ref):
    b, diag = place_ref[0], place_ref[1]
    ids = [r_ref[(n // 2) ^ b, pl.ds(MEMBERS * EXTRA + (n % 2) * IDS, IDS), :] for n in range(MEMBERS)]
    kt_ref[...] = jnp.concatenate(ids, axis=0).astype(F32).T
    spread_kinds(kt_ref, kb_ref, 0)

    def middle(n, carry):
        x = jnp.concatenate([r_ref[i ^ diag, pl.ds(pl.multiple_of(n * EXTRA, EXTRA), EXTRA), :] for i in range(NA)], axis=0)
        high = kb_ref[0, n]
        other = swap_halves(x)
        low = low_lanes()
        zero = jnp.zeros_like(x)
        rows = []
        for doubled in (jnp.where(low, x, other), jnp.where(low, other, x)):
            parts = []
            for j in (0, 2):
                first = jnp.where(high == float(j), doubled, zero)
                later = jnp.where(high == float(j + 1), doubled, zero)
                parts.append(jnp.where(low, first, later))
            rows.append(jnp.concatenate(parts, axis=1))
        prod = jnp.dot(jnp.concatenate(rows, axis=0), wmid_ref[...], preferred_element_type=F32)
        s_ref[1, n] = choose(prod[:CLUSTERS], prod[CLUSTERS:], kb_ref[1, n])
        return carry

    lax.fori_loop(0, MEMBERS, middle, 0)
    for l, mask in enumerate((8, 4, 2, 1)):
        spread_kinds(kt_ref, kb_ref, l + 1)

        def read(n, l=l):
            return s_ref[(l + 1) % 2, n]

        def write(n, value, l=l):
            if l == 3:
                out_ref[n] = value
            else:
                s_ref[l % 2, n] = value

        level(read, write, perm_ref[l], w_ref.at[l], kb_ref, mask, perm_ref[4] if l == 3 else None)


VMEM = pl.BlockSpec(memory_space=pltpu.VMEM)
SMEM = pl.BlockSpec(memory_space=pltpu.SMEM)
LIMIT = 40 * 1024 * 1024


def call(kernel, name, out_shape, in_specs, scratch=(), flops=0, count=0):
    many = isinstance(out_shape, tuple)
    return pl.pallas_call(
        kernel,
        out_shape=out_shape,
        in_specs=in_specs,
        out_specs=(VMEM,) * len(out_shape) if many else VMEM,
        scratch_shapes=list(scratch),
        compiler_params=pltpu.CompilerParams(vmem_limit_bytes=LIMIT),
        cost_estimate=pl.CostEstimate(flops=flops, bytes_accessed=count, transcendentals=0),
        name=name,
    )


def on_device(coefficients, src_blocks, mid_blocks, obs_blocks, block_ids, partner_perm, owner_order):
    a = lax.axis_index("gx")
    b = lax.axis_index("gy") // 2
    place = jnp.stack([b, a ^ b]).astype(jnp.int32)
    ordered = jnp.asarray(np.eye(CLUSTERS)[:, ORDER], BF)
    order = jnp.asarray(ORDER[None], F32)

    def shape(*dims):
        return jax.ShapeDtypeStruct(dims, BF)

    x = call(pack_kernel, "pack", shape(MEMBERS, CLUSTERS + EXTRA, LANES), [VMEM] * 4, count=2**21)(
        coefficients[0, 0], block_ids[0, 0], owner_order[0], ordered
    )
    x = lax.all_to_all(x, AXES, split_axis=0, concat_axis=0, tiled=True, axis_index_groups=SRC_GROUPS)
    square, wide = (CLUSTERS, CLUSTERS), (8 * HALF, 4 * HALF)
    src_perm, obs_perm, src_w, obs_w, mid_w = call(
        table_kernel,
        "tables",
        (shape(4, *square), shape(5, *square), shape(4, *wide), shape(4, *wide), shape(4 * HALF, 4 * HALF)),
        [VMEM] * 6,
        flops=10**9,
        count=2**24,
    )(src_blocks, mid_blocks, obs_blocks, partner_perm, ordered, order)

    ids = pltpu.VMEM((LANES, MEMBERS * IDS), F32)
    state = pltpu.VMEM((2, MEMBERS, CLUSTERS, LANES), BF)
    mid = call(
        source_kernel,
        "source_levels",
        shape(NA, (MEMBERS + 1) * EXTRA, LANES),
        [SMEM, VMEM, VMEM, VMEM],
        (ids, state, state, pltpu.VMEM((MEMBERS * CLUSTERS, LANES), F32)),
    )(place, x, src_perm, src_w)
    mid = lax.all_to_all(mid, AXES, split_axis=0, concat_axis=0, tiled=True, axis_index_groups=MID_GROUPS)
    done = call(
        observation_kernel,
        "observation_levels",
        shape(MEMBERS, CLUSTERS, LANES),
        [SMEM, VMEM, VMEM, VMEM, VMEM],
        (ids, state, state),
    )(place, mid, obs_perm, obs_w, mid_w)
    out = lax.all_to_all(
        done.reshape(MEMBERS * CLUSTERS, LANES),
        AXES,
        split_axis=0,
        concat_axis=1,
        tiled=True,
        axis_index_groups=OBS_GROUPS,
    )
    return out.reshape(1, 1, CLUSTERS, MEMBERS * LANES)


def solution(mesh):
    in_specs = (
        P("gy", "gx", None, None),
        P(),
        P(),
        P(),
        P("gy", "gx", None, None),
        P(),
        P("gy", "gx", None),
    )
    out_specs = P("gy", "gx", None, None)
    return jax.shard_map(on_device, mesh=mesh, in_specs=in_specs, out_specs=out_specs, check_vma=False)
```

profile of v0, /device:TPU:1, one launch (start us, length us, event | category | flops | bytes accessed | tf_op | source)
XLA Modules:
  0.0 143.6 jit_solution(3300811791578882284)
XLA Ops:
  0.0 0.8 copy.11
  0.8 0.0 copy-start.2
  0.8 1.2 copy-done.2
  2.0 0.0 copy-start.9
  2.0 0.9 copy-done.9
  2.9 0.0 copy-start.15
  2.9 0.7 copy-done.15
  3.6 1.3 pack.1
  4.9 0.0 copy-start
  4.9 0.0 copy-start.10
  4.9 0.0 copy-start.14
  4.9 0.0 copy-start.16
  4.9 7.1 %all-to-all-start = ((bf16[16,288,128]{2,1,0:T(8,128)(2,1)}), bf16[16,288,128]{2,1,0:T(8,128)(2,1)S(1)}, u32[]{:S(2)}, u32[]{:S(2)}) async-start(bf16[16,288,128]{2,1,0:T(8,128)(2,1)} %pack.1), calls=%async_computation | async-start | bytes 2359296 | tf_op jit(solution)/shard_map/all_to_all | solution.py:259
  12.0 0.0 copy-done
  12.0 0.0 copy-done.10
  12.0 0.0 copy-done.14
  12.0 0.0 copy-done.16
  12.0 0.0 copy-start.1
  12.0 1.6 %copy-done.1 = bf16[4,16,2,2,32,32]{5,4,3,2,1,0:T(8,128)(2,1)S(1)} copy-done((bf16[4,16,2,2,32,32]{5,4,3,2,1,0:T(8,128)(2,1)S(1)}, bf16[4,16,2,2,32,32]{5,4,3,2,1,0:T(8,128)(2,1)}, u32[]{:S(2)}) %copy-start.1) | copy-done | bytes 524312
  13.6 0.0 copy-start.13
  13.6 0.9 copy-done.13
  14.5 3.5 %tables.1 = (bf16[4,256,256]{2,1,0:T(8,128)(2,1)S(1)}, bf16[5,256,256]{2,1,0:T(8,128)(2,1)S(1)}, bf16[4,512,256]{2,1,0:T(8,128)(2,1)S(1)}, bf16[4,512,256]{2,1,0:T(8,128)(2,1)S(1)}, bf16[256,256]{1,0:T(8,128)(2,1)S(1)}) custom-call(bf16[4,16,2,2,32,32]{5,4,3,2,1,0:T(8,128)(2,1)S(1)} %copy-done, bf16[16,2,32,32]{3,2,1,0:T(8,128)(2,1)S(1)} %copy-done.13, ...), custom_call_target="tpu_custom_call" | custom-call | flops 1000000000 | bytes 16777216 | tf_op jit(solution)/shard_map/tables/pallas_call | solution.py:261
  18.0 0.0 copy-start.3
  18.0 0.9 copy-done.3
  19.0 0.0 copy-start.5
  19.0 1.0 copy-done.5
  20.0 0.0 copy-start.7
  20.0 0.8 copy-done.7
  20.8 0.0 copy-start.11
  20.8 0.8 copy-done.11
  21.6 0.1 pad_add_fusion.place_ref
  21.7 7.6 %all-to-all-done.x_ref = bf16[16,288,128]{2,1,0:T(8,128)(2,1)S(1)} async-done(((bf16[16,288,128]{2,1,0:T(8,128)(2,1)}), bf16[16,288,128]{2,1,0:T(8,128)(2,1)S(1)}, u32[]{:S(2)}, u32[]{:S(2)}) %all-to-all-start) | async-done | bytes 1179680 | tf_op jit(solution)/shard_map/all_to_all | solution.py:259
  29.3 0.0 copy-start.6
  29.3 1.2 copy-done.6
  30.5 0.0 copy-start.12
  30.5 1.0 copy-done.12
  31.5 28.7 %source_levels.1 = bf16[8,544,128]{2,1,0:T(8,128)(2,1)S(1)} custom-call(s32[2]{0:T(128)S(1)} %pad_add_fusion.place_ref, bf16[16,288,128]{2,1,0:T(8,128)(2,1)S(1)} %all-to-all-done.x_ref, bf16[4,256,256]{2,1,0:T(8,128)(2,1)S(1)} %copy-done.12, bf16[4,512,256]{2,1,0:T(8,128)(2,1)S(1)} %copy-done.6), custom_call_target="tpu_custom_call" | custom-call | tf_op jit(solution)/shard_map/source_levels/pallas_call | solution.py:272
  60.3 0.0 copy-start.4
  60.3 0.0 copy-start.8
  60.3 26.3 %all_to_all.23.r_ref = bf16[8,544,128]{2,1,0:T(8,128)(2,1)S(1)} all-to-all(bf16[8,544,128]{2,1,0:T(8,128)(2,1)S(1)} %source_levels.1), channel_id=1, replica_groups={{0,18,36,54,72,90,108,126},{1,19,37,55,73,91,109,127},{2,16,38,52,74,88..., dimensions={0} | all-to-all | bytes 2228224 | tf_op jit(solution)/shard_map/all_to_all | solution.py:279
  86.5 0.0 copy-done.4
  86.5 0.0 copy-done.8
  86.6 33.2 %observation_levels.1 = bf16[16,256,128]{2,1,0:T(8,128)(2,1)S(1)} custom-call(s32[2]{0:T(128)S(1)} %pad_add_fusion.place_ref, bf16[8,544,128]{2,1,0:T(8,128)(2,1)S(1)} %all_to_all.23.r_ref, bf16[5,256,256]{2,1,0:T(8,128)(2,1)S(1)} %copy-done.8, bf16[4,512,256]{2,1,0:T(8,128)(2,1)S(1)} %copy-done.4, bf16[256,256]{1,0:T(8,128)(2,1)S(1)} %get-tuple-element.14.wmid_ref), custom_call_target="tpu_custom_call" | custom-call | tf_op jit(solution)/shard_map/observation_levels/pallas_call | solution.py:280
  119.7 22.0 %all_to_all.24 = bf16[16,256,128]{2,1,0:T(8,128)(2,1)S(1)} all-to-all(bf16[16,256,128]{2,1,0:T(8,128)(2,1)S(1)} %observation_levels.1), channel_id=1, replica_groups={{0,1,2,3,4,5,6,7,8,9,10,11,12,13,14,15},{18,19,16,17,22,23,20,21,26,27,..., dimensions={0} | all-to-all | bytes 2097152 | tf_op jit(solution)/shard_map/all_to_all | solution.py:287
  141.7 0.5 copy.12
  142.2 1.4 copy.13
Async XLA Ops:
  0.8 1.2 copy-start.2
  2.0 0.9 copy-start.9
  2.9 0.7 copy-start.15
  4.9 7.1 %copy-start = (bf16[4,16,2,2,32,32]{5,4,3,2,1,0:T(8,128)(2,1)S(1)}, bf16[4,16,2,2,32,32]{5,4,3,2,1,0:T(8,128)(2,1)}, u32[]{:S(2)}) copy-start(bf16[4,16,2,2,32,32]{5,4,3,2,1,0:T(8,128)(2,1)} %src_ref.1) | copy-start | bytes 1572868
  4.9 7.1 %copy-start.10 = (bf16[256,256]{1,0:T(8,128)(2,1)S(1)}, bf16[256,256]{1,0:T(8,128)(2,1)}, u32[]{:S(2)}) copy-start(bf16[256,256]{1,0:T(8,128)(2,1)} %constant.27.clone.ordered_ref) | copy-start | bytes 393220
  4.9 7.1 %copy-start.14 = (s32[8,256]{1,0:T(8,128)S(1)}, s32[8,256]{1,0:T(8,128)}, u32[]{:S(2)}) copy-start(s32[8,256]{1,0:T(8,128)} %perm_ref.1) | copy-start | bytes 24580
  4.9 7.1 %copy-start.16 = (f32[1,256]{1,0:T(1,128)S(1)}, f32[1,256]{1,0:T(1,128)}, u32[]{:S(2)}) copy-start(f32[1,256]{1,0:T(1,128)} %constant.28.clone.order_ref) | copy-start | bytes 3076
  4.9 24.3 %all-to-all-start = ((bf16[16,288,128]{2,1,0:T(8,128)(2,1)}), bf16[16,288,128]{2,1,0:T(8,128)(2,1)S(1)}, u32[]{:S(2)}, u32[]{:S(2)}) async-start(bf16[16,288,128]{2,1,0:T(8,128)(2,1)} %pack.1), calls=%async_computation | async-start | bytes 2359296 | tf_op jit(solution)/shard_map/all_to_all | solution.py:259
  12.0 1.6 %copy-start.1 = (bf16[4,16,2,2,32,32]{5,4,3,2,1,0:T(8,128)(2,1)S(1)}, bf16[4,16,2,2,32,32]{5,4,3,2,1,0:T(8,128)(2,1)}, u32[]{:S(2)}) copy-start(bf16[4,16,2,2,32,32]{5,4,3,2,1,0:T(8,128)(2,1)} %obs_ref.1) | copy-start | bytes 1572868
  13.6 0.9 copy-start.13
  18.0 0.9 copy-start.3
  19.0 1.0 copy-start.5
  20.0 0.8 copy-start.7
  20.8 0.8 copy-start.11
  29.3 1.2 copy-start.6
  30.5 1.0 copy-start.12
  60.3 26.3 %copy-start.4 = (bf16[4,512,256]{2,1,0:T(8,128)(2,1)S(1)}, bf16[4,512,256]{2,1,0:T(8,128)(2,1)}, u32[]{:S(2)}) copy-start(bf16[4,512,256]{2,1,0:T(8,128)(2,1)} %copy-done.3) | copy-start | bytes 3145732
  60.3 26.3 %copy-start.8 = (bf16[5,256,256]{2,1,0:T(8,128)(2,1)S(1)}, bf16[5,256,256]{2,1,0:T(8,128)(2,1)}, u32[]{:S(2)}) copy-start(bf16[5,256,256]{2,1,0:T(8,128)(2,1)} %copy-done.7) | copy-start | bytes 1966084
where the time goes:
time: 144 us
  Pallas kernels  66.7 us (46%)
  blocking collectives  48.2 us (33%)
  local copies, waits for them, and re-layouts  13.9 us (10%)
  waiting for transfers between devices  7.59 us (5%)
  starting transfers between devices  7.06 us (5%)
    pallas_call x1, Pallas kernels, on_device(): call(observation_kernel, 'observation_levels', shape(MEMBERS, CLUSTERS, L...  33.2 us
    pallas_call x1, Pallas kernels, on_device(): call(source_kernel, 'source_levels', shape(NA, (MEMBERS + 1) * EXTRA, LAN...  28.7 us
    all_to_all x1, blocking collectives, on_device(): lax.all_to_all(mid, AXES, split_axis=0, concat_axis=0, tiled=True, axis_i...  26.3 us
    all_to_all x1, blocking collectives, on_device(): lax.all_to_all(done.reshape(MEMBERS * CLUSTERS, LANES), AXES, split_axis=...  22 us
    unnamed x35, local copies, waits for them, and re-layouts  12 us
    all_to_all x1, waiting for transfers between devices, on_device(): lax.all_to_all(x, AXES, split_axis=0, concat_axis=0, tiled=True, axis_ind...  7.59 us
    all_to_all x1, starting transfers between devices, on_device(): lax.all_to_all(x, AXES, split_axis=0, concat_axis=0, tiled=True, axis_ind...  7.06 us
    pallas_call x1, Pallas kernels, on_device(): call(table_kernel, 'tables', (shape(4, *square), shape(5, *square), shape...  3.49 us
  transfers between devices with their start and end apart: 1, of which 1 were waited for; matrix products, arithmetic and copies ran while one was open for 0% of the time, Pallas kernels for 2%

commit v1 on v0

--- a/solution.py
+++ b/solution.py
@@ -51,14 +51,17 @@
         out_ref[t, CLUSTERS:, :] = extra
 
 
-def turned_weights(block, parts):
+def turned_weights(block, parts, lows):
     rows = []
-    for low in range(4):
-        each = [(4 * high + low, part) for high in range(4) for part in range(parts)]
+    for low in lows:
+        each = [(4 * high + low, part) for high in range(4) for part in parts]
         top = [(block(k, p, 0), -block(k, p, 1)) for k, p in each]
         bottom = [(block(k, p, 1), block(k, p, 0)) for k, p in each]
         rows += [jnp.concatenate([piece for pair in half for piece in pair], axis=1) for half in (top, bottom)]
     return jnp.concatenate(rows, axis=0).T.astype(BF)
+
+
+FORMS = (((0, 1), (0, 1, 2, 3)), ((1, 0), (1, 0, 3, 2)))
 
 
 def table_kernel(
@@ -82,12 +85,14 @@
     obs_perm_ref[4] = match(lax.broadcasted_iota(jnp.int32, shape, 0).astype(F32), order)
 
     def weights(l, carry):
-        src_w_ref[l] = turned_weights(lambda k, p, i: src_ref[l, k, p, i].astype(F32), 2)
-        obs_w_ref[l] = turned_weights(lambda k, p, i: obs_ref[l, k, p, i].astype(F32), 2)
+        for form, (parts, lows) in enumerate(FORMS):
+            src_w_ref[l, form] = turned_weights(lambda k, p, i: src_ref[l, k, p, i].astype(F32), parts, lows)
+            obs_w_ref[l, form] = turned_weights(lambda k, p, i: obs_ref[l, k, p, i].astype(F32), parts, lows)
         return carry
 
     lax.fori_loop(0, 4, weights, 0)
-    mid_w_ref[...] = turned_weights(lambda k, p, i: mid_ref[k, i].astype(F32), 1)
+    for form, (_, lows) in enumerate(FORMS):
+        mid_w_ref[form] = turned_weights(lambda k, p, i: mid_ref[k, i].astype(F32), (0,), lows)
 
 
 def spread_kinds(kt_ref, kb_ref, row):
@@ -96,27 +101,20 @@
             col = m * IDS + 8 * half + row
             kinds = jnp.broadcast_to(kt_ref[:, col : col + 1], (LANES, LANES))
             high = jnp.floor(kinds * 0.25)
+            low = kinds - 4.0 * high
+            second = jnp.floor(low * 0.5)
             at = slice(half * LANES, (half + 1) * LANES)
             kb_ref[0, m, at, :] = high.astype(BF)
-            kb_ref[1, m, at, :] = (kinds - 4.0 * high).astype(BF)
-
-
-def swap_halves(x):
-    return jnp.concatenate([x[:, HALF:], x[:, :HALF]], axis=1)
-
-
-def low_lanes():
-    return lax.broadcasted_iota(jnp.int32, (CLUSTERS, LANES), 1) < HALF
-
-
-def choose(prod_u, prod_v, low):
-    second = low >= 2.0
-    odd = (low == 1.0) | (low == 3.0)
-    fu = jnp.where(second, prod_u[:, LANES:].astype(BF), prod_u[:, :LANES].astype(BF))
-    fv = jnp.where(second, prod_v[:, LANES:].astype(BF), prod_v[:, :LANES].astype(BF))
-    left = jnp.where(odd, swap_halves(fu), fu)
-    right = jnp.where(odd, fv, swap_halves(fv))
-    return jnp.concatenate([left[:, :HALF], right[:, HALF:]], axis=1)
+            kb_ref[1, m, at, :] = second.astype(BF)
+            kb_ref[2, m, at, :] = (low - 2.0 * second).astype(BF)
+
+
+def first_side():
+    return lax.broadcasted_iota(jnp.int32, (CLUSTERS, LANES), 1).astype(F32).astype(BF) < HALF
+
+
+def other_side(x):
+    return pltpu.roll(x, HALF, 1)
 
 
 def expand(x, high):
@@ -124,31 +122,52 @@
     return jnp.concatenate([jnp.where(high == float(j), x, zero) for j in range(4)], axis=1)
 
 
-def level(read, write, perm, weights, kb_ref, mask, own_perm=None):
+def expand_halves(x, high, first):
+    zero = jnp.zeros_like(x)
+    parts = []
+    for j in (0, 2):
+        parts.append(jnp.where(first, jnp.where(high == float(j), x, zero), jnp.where(high == float(j + 1), x, zero)))
+    return jnp.concatenate(parts, axis=1)
+
+
+def multiply(ms, rows, weights, kb_ref, write, first):
+    prods = [
+        jnp.dot(jnp.concatenate([r[side] for r in rows], axis=0), weights[side], preferred_element_type=F32)
+        for side in range(2)
+    ]
+    for k, m in enumerate(ms):
+        second, odd = kb_ref[1, m] > 0.5, kb_ref[2, m] > 0.5
+        at = slice(k * CLUSTERS, (k + 1) * CLUSTERS)
+        one, two = [jnp.where(second, p[at, LANES:].astype(BF), p[at, :LANES].astype(BF)) for p in prods]
+        kept = jnp.where(jnp.logical_xor(first, odd), one, two)
+        turned = other_side(kept)
+        write(m, jnp.where(odd, turned, kept), jnp.where(odd, kept, turned))
+
+
+BATCH = 8
+
+
+def level(read, read_turned, write, perm, weights, kb_ref, mask, own_perm=None):
     def body(i, carry):
-        ms = [2 * i, 2 * i + 1]
-        far = jnp.concatenate([read(m ^ mask) for m in ms], axis=1)
+        first = first_side()
+        ms = [BATCH * i + k for k in range(BATCH)]
+        far = jnp.concatenate([read_turned(m ^ mask) for m in ms], axis=1)
         far = jnp.dot(perm, far, preferred_element_type=F32).astype(BF)
-        own = jnp.concatenate([read(m) for m in ms], axis=1)
+        own = [read(m) for m in ms]
         if own_perm is not None:
-            own = jnp.dot(own_perm, own, preferred_element_type=F32).astype(BF)
+            own = jnp.dot(own_perm, jnp.concatenate(own, axis=1), preferred_element_type=F32).astype(BF)
+            own = [own[:, k * LANES : (k + 1) * LANES] for k in range(BATCH)]
         rows = []
         for k, m in enumerate(ms):
-            x = own[:, k * LANES : (k + 1) * LANES]
-            y = far[:, k * LANES : (k + 1) * LANES]
-            high = kb_ref[0, m]
-            rows.append(expand(jnp.concatenate([x[:, :HALF], y[:, :HALF]], axis=1), high))
-            rows.append(expand(jnp.concatenate([x[:, HALF:], y[:, HALF:]], axis=1), high))
-        prod = jnp.dot(jnp.concatenate(rows, axis=0), weights[...], preferred_element_type=F32)
-        for k, m in enumerate(ms):
-            at = 2 * k * CLUSTERS
-            write(m, choose(prod[at : at + CLUSTERS], prod[at + CLUSTERS : at + 2 * CLUSTERS], kb_ref[1, m]))
+            x, y, high = own[k], far[:, k * LANES : (k + 1) * LANES], kb_ref[0, m]
+            rows.append((expand(jnp.where(first, x, y), high), expand(jnp.where(first, y, x), high)))
+        multiply(ms, rows, weights, kb_ref, write, first)
         return carry
 
-    lax.fori_loop(0, MEMBERS // 2, body, 0)
-
-
-def source_kernel(place_ref, x_ref, perm_ref, w_ref, out_ref, kt_ref, kb_ref, s_ref, f_ref):
+    lax.fori_loop(0, MEMBERS // BATCH, body, 0)
+
+
+def source_kernel(place_ref, x_ref, perm_ref, w_ref, out_ref, kt_ref, kb_ref, s_ref, t_ref, f_ref):
     b = place_ref[0]
     kt_ref[...] = x_ref[:, CLUSTERS : CLUSTERS + IDS, :].reshape(MEMBERS * IDS, LANES).astype(F32).T
     for l, mask in enumerate((2, 4, 8, 1)):
@@ -157,10 +176,14 @@
         def read(m, l=l):
             return x_ref[m, :CLUSTERS, :] if l == 0 else s_ref[(l - 1) % 2, m]
 
-        def write(m, value, l=l):
+        def read_turned(m, l=l):
+            return other_side(x_ref[m, :CLUSTERS, :]) if l == 0 else t_ref[(l - 1) % 2, m]
+
+        def write(m, value, turned, l=l):
             s_ref[l % 2, m] = value
-
-        level(read, write, perm_ref[l], w_ref.at[l], kb_ref, mask)
+            t_ref[l % 2, m] = turned
+
+        level(read, read_turned, write, perm_ref[l], w_ref.at[l], kb_ref, mask)
     lane = lax.broadcasted_iota(jnp.int32, (LANES, LANES), 1).astype(F32)
     for m in range(MEMBERS):
         picks = []
@@ -184,44 +207,47 @@
             out_ref[h, at : at + IDS, :] = x_ref[(h ^ b) * 2 + c, CLUSTERS + IDS :, :]
 
 
-def observation_kernel(place_ref, r_ref, perm_ref, w_ref, wmid_ref, out_ref, kt_ref, kb_ref, s_ref):
+def observation_kernel(place_ref, r_ref, perm_ref, w_ref, wmid_ref, out_ref, kt_ref, kb_ref, s_ref, t_ref):
     b, diag = place_ref[0], place_ref[1]
     ids = [r_ref[(n // 2) ^ b, pl.ds(MEMBERS * EXTRA + (n % 2) * IDS, IDS), :] for n in range(MEMBERS)]
     kt_ref[...] = jnp.concatenate(ids, axis=0).astype(F32).T
     spread_kinds(kt_ref, kb_ref, 0)
 
-    def middle(n, carry):
-        x = jnp.concatenate([r_ref[i ^ diag, pl.ds(pl.multiple_of(n * EXTRA, EXTRA), EXTRA), :] for i in range(NA)], axis=0)
-        high = kb_ref[0, n]
-        other = swap_halves(x)
-        low = low_lanes()
-        zero = jnp.zeros_like(x)
+    def put(slot):
+        def write(n, value, turned):
+            s_ref[slot, n] = value
+            t_ref[slot, n] = turned
+
+        return write
+
+    def middle(i, carry):
+        first = first_side()
+        ns = [BATCH * i + k for k in range(BATCH)]
         rows = []
-        for doubled in (jnp.where(low, x, other), jnp.where(low, other, x)):
-            parts = []
-            for j in (0, 2):
-                first = jnp.where(high == float(j), doubled, zero)
-                later = jnp.where(high == float(j + 1), doubled, zero)
-                parts.append(jnp.where(low, first, later))
-            rows.append(jnp.concatenate(parts, axis=1))
-        prod = jnp.dot(jnp.concatenate(rows, axis=0), wmid_ref[...], preferred_element_type=F32)
-        s_ref[1, n] = choose(prod[:CLUSTERS], prod[CLUSTERS:], kb_ref[1, n])
+        for n in ns:
+            at = pl.ds(pl.multiple_of(n * EXTRA, EXTRA), EXTRA)
+            x = jnp.concatenate([r_ref[j ^ diag, at, :] for j in range(NA)], axis=0)
+            turned, high = other_side(x), kb_ref[0, n]
+            one, two = jnp.where(first, x, turned), jnp.where(first, turned, x)
+            rows.append((expand_halves(one, high, first), expand_halves(two, high, first)))
+        multiply(ns, rows, wmid_ref, kb_ref, put(1), first)
         return carry
 
-    lax.fori_loop(0, MEMBERS, middle, 0)
+    lax.fori_loop(0, MEMBERS // BATCH, middle, 0)
     for l, mask in enumerate((8, 4, 2, 1)):
         spread_kinds(kt_ref, kb_ref, l + 1)
 
         def read(n, l=l):
             return s_ref[(l + 1) % 2, n]
 
-        def write(n, value, l=l):
-            if l == 3:
-                out_ref[n] = value
-            else:
-                s_ref[l % 2, n] = value
-
-        level(read, write, perm_ref[l], w_ref.at[l], kb_ref, mask, perm_ref[4] if l == 3 else None)
+        def read_turned(n, l=l):
+            return t_ref[(l + 1) % 2, n]
+
+        def last(n, value, turned):
+            out_ref[n] = value
+
+        write = last if l == 3 else put(l % 2)
+        level(read, read_turned, write, perm_ref[l], w_ref.at[l], kb_ref, mask, perm_ref[4] if l == 3 else None)
 
 
 VMEM = pl.BlockSpec(memory_space=pltpu.VMEM)
@@ -257,11 +283,11 @@
         coefficients[0, 0], block_ids[0, 0], owner_order[0], ordered
     )
     x = lax.all_to_all(x, AXES, split_axis=0, concat_axis=0, tiled=True, axis_index_groups=SRC_GROUPS)
-    square, wide = (CLUSTERS, CLUSTERS), (8 * HALF, 4 * HALF)
+    square, wide = (CLUSTERS, CLUSTERS), (2, 8 * HALF, 4 * HALF)
     src_perm, obs_perm, src_w, obs_w, mid_w = call(
         table_kernel,
         "tables",
-        (shape(4, *square), shape(5, *square), shape(4, *wide), shape(4, *wide), shape(4 * HALF, 4 * HALF)),
+        (shape(4, *square), shape(5, *square), shape(4, *wide), shape(4, *wide), shape(2, 4 * HALF, 4 * HALF)),
         [VMEM] * 6,
         flops=10**9,
         count=2**24,
@@ -269,12 +295,13 @@
 
     ids = pltpu.VMEM((LANES, MEMBERS * IDS), F32)
     state = pltpu.VMEM((2, MEMBERS, CLUSTERS, LANES), BF)
+    kinds = pltpu.VMEM((3, MEMBERS, CLUSTERS, LANES), BF)
     mid = call(
         source_kernel,
         "source_levels",
         shape(NA, (MEMBERS + 1) * EXTRA, LANES),
         [SMEM, VMEM, VMEM, VMEM],
-        (ids, state, state, pltpu.VMEM((MEMBERS * CLUSTERS, LANES), F32)),
+        (ids, kinds, state, state, pltpu.VMEM((MEMBERS * CLUSTERS, LANES), F32)),
     )(place, x, src_perm, src_w)
     mid = lax.all_to_all(mid, AXES, split_axis=0, concat_axis=0, tiled=True, axis_index_groups=MID_GROUPS)
     done = call(
@@ -282,7 +309,7 @@
         "observation_levels",
         shape(MEMBERS, CLUSTERS, LANES),
         [SMEM, VMEM, VMEM, VMEM, VMEM],
-        (ids, state, state),
+        (ids, kinds, state, state),
     )(place, mid, obs_perm, obs_w, mid_w)
     out = lax.all_to_all(
         done.reshape(MEMBERS * CLUSTERS, LANES),

time: 144 us -> 127 us (0.88)
  Pallas kernels: 66.7 us -> 52 us
  waiting for transfers between devices: 7.59 us -> 3.78 us
  local copies, waits for them, and re-layouts: 13.9 us -> 15.7 us
    pallas_call x1, Pallas kernels: 33.2 us -> 23.3 us  [on_device(): call(observation_kernel, 'observation_levels', shape(MEMBERS, CLUSTERS, L...]
    pallas_call x1, Pallas kernels: 28.7 us -> 21.6 us  [on_device(): call(source_kernel, 'source_levels', shape(NA, (MEMBERS + 1) * EXTRA, LAN...]
    all_to_all x1, waiting for transfers between devices: 7.59 us -> 3.78 us  [on_device(): lax.all_to_all(x, AXES, split_axis=0, concat_axis=0, tiled=True, axis_ind...]
    pallas_call x1, Pallas kernels: 3.49 us -> 5.87 us  [on_device(): call(table_kernel, 'tables', (shape(4, *square), shape(5, *square), shape...]
    unnamed x35 -> x39, local copies, waits for them, and re-layouts: 12 us -> 13.8 us
  transfers between devices with their start and end apart: 1 -> 1, of which waited for: 1 -> 1; matrix products, arithmetic and copies ran while one was open for 0% -> 0% of each run, Pallas kernels for 2% -> 5%
where the time goes in v1:
time: 127 us
  Pallas kernels  52 us (41%)
  blocking collectives  48.3 us (38%)
  local copies, waits for them, and re-layouts  15.7 us (12%)
  starting transfers between devices  6.91 us (5%)
  waiting for transfers between devices  3.78 us (3%)
    all_to_all x1, blocking collectives, on_device(): lax.all_to_all(mid, AXES, split_axis=0, concat_axis=0, tiled=True, axis_i...  26.3 us
    pallas_call x1, Pallas kernels, on_device(): call(observation_kernel, 'observation_levels', shape(MEMBERS, CLUSTERS, L...  23.3 us
    all_to_all x1, blocking collectives, on_device(): lax.all_to_all(done.reshape(MEMBERS * CLUSTERS, LANES), AXES, split_axis=...  22 us
    pallas_call x1, Pallas kernels, on_device(): call(source_kernel, 'source_levels', shape(NA, (MEMBERS + 1) * EXTRA, LAN...  21.6 us
    unnamed x39, local copies, waits for them, and re-layouts  13.8 us
    all_to_all x1, starting transfers between devices, on_device(): lax.all_to_all(x, AXES, split_axis=0, concat_axis=0, tiled=True, axis_ind...  6.91 us
    pallas_call x1, Pallas kernels, on_device(): call(table_kernel, 'tables', (shape(4, *square), shape(5, *square), shape...  5.87 us
    all_to_all x1, waiting for transfers between devices, on_device(): lax.all_to_all(x, AXES, split_axis=0, concat_axis=0, tiled=True, axis_ind...  3.78 us
  transfers between devices with their start and end apart: 1, of which 1 were waited for; matrix products, arithmetic and copies ran while one was open for 0% of the time, Pallas kernels for 5%

profile of v1, /device:TPU:1, one launch (start us, length us, event | category | flops | bytes accessed | tf_op | source)
XLA Modules:
  0.0 126.9 jit_solution(1423741135062906590)
XLA Ops:
  0.0 0.8 copy.11
  0.8 0.0 copy-start.6
  0.8 1.2 copy-done.6
  2.0 0.0 copy-start.11
  2.0 0.9 copy-done.11
  2.9 0.0 copy-start.17
  2.9 0.7 copy-done.17
  3.6 0.0 copy-start
  3.6 0.0 copy-start.12
  3.6 0.0 copy-start.16
  3.6 0.0 copy-start.18
  3.6 1.3 pack.1
  4.9 6.9 %all-to-all-start = ((bf16[16,288,128]{2,1,0:T(8,128)(2,1)}), bf16[16,288,128]{2,1,0:T(8,128)(2,1)S(1)}, u32[]{:S(2)}, u32[]{:S(2)}) async-start(bf16[16,288,128]{2,1,0:T(8,128)(2,1)} %pack.1), calls=%async_computation | async-start | bytes 2359296 | tf_op jit(solution)/shard_map/all_to_all | solution.py:285
  11.8 0.0 copy-done
  11.8 0.0 copy-done.12
  11.8 0.0 copy-done.16
  11.8 0.0 copy-done.18
  11.8 0.0 copy-start.1
  11.9 1.6 %copy-done.1 = bf16[4,16,2,2,32,32]{5,4,3,2,1,0:T(8,128)(2,1)S(1)} copy-done((bf16[4,16,2,2,32,32]{5,4,3,2,1,0:T(8,128)(2,1)S(1)}, bf16[4,16,2,2,32,32]{5,4,3,2,1,0:T(8,128)(2,1)}, u32[]{:S(2)}) %copy-start.1) | copy-done | bytes 524312
  13.4 0.0 copy-start.13
  13.4 0.9 copy-done.13
  14.4 5.9 %tables.1 = (bf16[4,256,256]{2,1,0:T(8,128)(2,1)S(1)}, bf16[5,256,256]{2,1,0:T(8,128)(2,1)S(1)}, bf16[4,2,512,256]{3,2,1,0:T(8,128)(2,1)S(1)}, bf16[4,2,512,256]...) custom-call(bf16[4,16,2,2,32,32]{5,4,3,2,1,0:T(8,128)(2,1)S(1)} %copy-done, bf16[16,2,32,32]{3,2,1,0:T(8,128)(2,1)S(1)} %copy-done.13, ...), custom_call_target="tpu_custom_call" | custom-call | flops 1000000000 | bytes 16777216 | tf_op jit(solution)/shard_map/tables/pallas_call | solution.py:287
  20.3 0.0 copy-start.2
  20.3 1.3 %copy-done.2 = bf16[4,2,512,256]{3,2,1,0:T(8,128)(2,1)} copy-done((bf16[4,2,512,256]{3,2,1,0:T(8,128)(2,1)}, bf16[4,2,512,256]{3,2,1,0:T(8,128)(2,1)S(1)}, u32[]{:S(2)}) %copy-start.2) | copy-done | bytes 2097176
  21.6 0.0 copy-start.4
  21.6 1.3 %copy-done.4 = bf16[4,2,512,256]{3,2,1,0:T(8,128)(2,1)} copy-done((bf16[4,2,512,256]{3,2,1,0:T(8,128)(2,1)}, bf16[4,2,512,256]{3,2,1,0:T(8,128)(2,1)S(1)}, u32[]{:S(2)}) %copy-start.4) | copy-done | bytes 2097176
  22.9 0.0 copy-start.7
  22.9 0.8 copy-done.7
  23.7 0.0 copy-start.9
  23.7 0.8 copy-done.9
  24.5 0.0 copy-start.14
  24.5 0.7 copy-done.14
  25.2 0.1 pad_add_fusion.place_ref
  25.3 3.8 %all-to-all-done.x_ref = bf16[16,288,128]{2,1,0:T(8,128)(2,1)S(1)} async-done(((bf16[16,288,128]{2,1,0:T(8,128)(2,1)}), bf16[16,288,128]{2,1,0:T(8,128)(2,1)S(1)}, u32[]{:S(2)}, u32[]{:S(2)}) %all-to-all-start) | async-done | bytes 1179680 | tf_op jit(solution)/shard_map/all_to_all | solution.py:285
  29.1 0.0 copy-start.3
  29.1 1.6 %copy-done.3 = bf16[4,2,512,256]{3,2,1,0:T(8,128)(2,1)S(1)} copy-done((bf16[4,2,512,256]{3,2,1,0:T(8,128)(2,1)S(1)}, bf16[4,2,512,256]{3,2,1,0:T(8,128)(2,1)}, u32[]{:S(2)}) %copy-start.3) | copy-done | bytes 2097176
  30.7 0.0 copy-start.10
  30.7 1.0 copy-done.10
  31.7 21.6 %source_levels.1 = bf16[8,544,128]{2,1,0:T(8,128)(2,1)S(1)} custom-call(s32[2]{0:T(128)S(1)} %pad_add_fusion.place_ref, bf16[16,288,128]{2,1,0:T(8,128)(2,1)S(1)} %all-to-all-done.x_ref, bf16[4,256,256]{2,1,0:T(8,128)(2,1)S(1)} %copy-done.10, bf16[4,2,512,256]{3,2,1,0:T(8,128)(2,1)S(1)} %copy-done.3), custom_call_target="tpu_custom_call" | custom-call | tf_op jit(solution)/shard_map/source_levels/pallas_call | solution.py:299
  53.4 0.0 copy-start.5
  53.4 26.3 %all_to_all.23.r_ref = bf16[8,544,128]{2,1,0:T(8,128)(2,1)S(1)} all-to-all(bf16[8,544,128]{2,1,0:T(8,128)(2,1)S(1)} %source_levels.1), channel_id=1, replica_groups={{0,18,36,54,72,90,108,126},{1,19,37,55,73,91,109,127},{2,16,38,52,74,88..., dimensions={0} | all-to-all | bytes 2228224 | tf_op jit(solution)/shard_map/all_to_all | solution.py:306
  79.7 0.0 copy-done.8
  79.7 0.0 copy-done.15
  79.7 0.0 copy-done.5
  79.7 23.3 %observation_levels.1 = bf16[16,256,128]{2,1,0:T(8,128)(2,1)S(1)} custom-call(s32[2]{0:T(128)S(1)} %pad_add_fusion.place_ref, bf16[8,544,128]{2,1,0:T(8,128)(2,1)S(1)} %all_to_all.23.r_ref, bf16[5,256,256]{2,1,0:T(8,128)(2,1)S(1)} %copy-done.8, bf16[4,2,512,256]{3,2,1,0:T(8,128)(2,1)S(1)} %copy-done.5, bf16[2,256,256]{2,1,0:T(8,128)(2,1)S(1)} %copy-done.15), custom_call_target="tpu_custom_call" | custom-call | tf_op jit(solution)/shard_map/observation_levels/pallas_call | solution.py:307
  103.0 22.0 %all_to_all.24 = bf16[16,256,128]{2,1,0:T(8,128)(2,1)S(1)} all-to-all(bf16[16,256,128]{2,1,0:T(8,128)(2,1)S(1)} %observation_levels.1), channel_id=1, replica_groups={{0,1,2,3,4,5,6,7,8,9,10,11,12,13,14,15},{18,19,16,17,22,23,20,21,26,27,..., dimensions={0} | all-to-all | bytes 2097152 | tf_op jit(solution)/shard_map/all_to_all | solution.py:314
  125.0 0.5 copy.12
  125.5 1.4 %copy.13 = bf16[1,1,256,2048]{3,2,1,0:T(8,128)(2,1)} copy(bf16[1,1,256,2048]{2,3,1,0:T(8,128)(2,1)S(1)} %bitcast.11) | data formatting | bytes 2097152 | tf_op jit(solution)/shard_map/reshape | solution.py:322
  (2 shorter events, 0.0 us)
Async XLA Ops:
  0.8 1.2 copy-start.6
  2.0 0.9 copy-start.11
  2.9 0.7 copy-start.17
  3.6 8.2 %copy-start = (bf16[4,16,2,2,32,32]{5,4,3,2,1,0:T(8,128)(2,1)S(1)}, bf16[4,16,2,2,32,32]{5,4,3,2,1,0:T(8,128)(2,1)}, u32[]{:S(2)}) copy-start(bf16[4,16,2,2,32,32]{5,4,3,2,1,0:T(8,128)(2,1)} %src_ref.1) | copy-start | bytes 1572868
  3.6 8.2 %copy-start.12 = (bf16[256,256]{1,0:T(8,128)(2,1)S(1)}, bf16[256,256]{1,0:T(8,128)(2,1)}, u32[]{:S(2)}) copy-start(bf16[256,256]{1,0:T(8,128)(2,1)} %constant.27.clone.ordered_ref) | copy-start | bytes 393220
  3.6 8.2 %copy-start.16 = (s32[8,256]{1,0:T(8,128)S(1)}, s32[8,256]{1,0:T(8,128)}, u32[]{:S(2)}) copy-start(s32[8,256]{1,0:T(8,128)} %perm_ref.1) | copy-start | bytes 24580
  3.6 8.2 %copy-start.18 = (f32[1,256]{1,0:T(1,128)S(1)}, f32[1,256]{1,0:T(1,128)}, u32[]{:S(2)}) copy-start(f32[1,256]{1,0:T(1,128)} %constant.28.clone.order_ref) | copy-start | bytes 3076
  4.9 24.2 %all-to-all-start = ((bf16[16,288,128]{2,1,0:T(8,128)(2,1)}), bf16[16,288,128]{2,1,0:T(8,128)(2,1)S(1)}, u32[]{:S(2)}, u32[]{:S(2)}) async-start(bf16[16,288,128]{2,1,0:T(8,128)(2,1)} %pack.1), calls=%async_computation | async-start | bytes 2359296 | tf_op jit(solution)/shard_map/all_to_all | solution.py:285
  11.8 1.6 %copy-start.1 = (bf16[4,16,2,2,32,32]{5,4,3,2,1,0:T(8,128)(2,1)S(1)}, bf16[4,16,2,2,32,32]{5,4,3,2,1,0:T(8,128)(2,1)}, u32[]{:S(2)}) copy-start(bf16[4,16,2,2,32,32]{5,4,3,2,1,0:T(8,128)(2,1)} %obs_ref.1) | copy-start | bytes 1572868
  13.4 0.9 copy-start.13
  20.3 1.3 %copy-start.2 = (bf16[4,2,512,256]{3,2,1,0:T(8,128)(2,1)}, bf16[4,2,512,256]{3,2,1,0:T(8,128)(2,1)S(1)}, u32[]{:S(2)}) copy-start(bf16[4,2,512,256]{3,2,1,0:T(8,128)(2,1)S(1)} %get-tuple-element.11.w_ref) | copy-start | bytes 6291460
  21.6 1.3 %copy-start.4 = (bf16[4,2,512,256]{3,2,1,0:T(8,128)(2,1)}, bf16[4,2,512,256]{3,2,1,0:T(8,128)(2,1)S(1)}, u32[]{:S(2)}) copy-start(bf16[4,2,512,256]{3,2,1,0:T(8,128)(2,1)S(1)} %get-tuple-element.13.w_ref) | copy-start | bytes 6291460
  22.9 0.8 copy-start.7
  23.7 0.8 copy-start.9
  24.5 0.7 copy-start.14
  29.1 1.6 %copy-start.3 = (bf16[4,2,512,256]{3,2,1,0:T(8,128)(2,1)S(1)}, bf16[4,2,512,256]{3,2,1,0:T(8,128)(2,1)}, u32[]{:S(2)}) copy-start(bf16[4,2,512,256]{3,2,1,0:T(8,128)(2,1)} %copy-done.2) | copy-start | bytes 6291460
  30.7 1.0 copy-start.10
  31.7 48.0 %copy-start.8 = (bf16[5,256,256]{2,1,0:T(8,128)(2,1)S(1)}, bf16[5,256,256]{2,1,0:T(8,128)(2,1)}, u32[]{:S(2)}) copy-start(bf16[5,256,256]{2,1,0:T(8,128)(2,1)} %copy-done.7) | copy-start | bytes 1966084
  31.7 48.0 %copy-start.15 = (bf16[2,256,256]{2,1,0:T(8,128)(2,1)S(1)}, bf16[2,256,256]{2,1,0:T(8,128)(2,1)}, u32[]{:S(2)}) copy-start(bf16[2,256,256]{2,1,0:T(8,128)(2,1)} %copy-done.14) | copy-start | bytes 786436
  53.4 26.3 %copy-start.5 = (bf16[4,2,512,256]{3,2,1,0:T(8,128)(2,1)S(1)}, bf16[4,2,512,256]{3,2,1,0:T(8,128)(2,1)}, u32[]{:S(2)}) copy-start(bf16[4,2,512,256]{3,2,1,0:T(8,128)(2,1)} %copy-done.4) | copy-start | bytes 6291460

commit v2 on v1

--- a/solution.py
+++ b/solution.py
@@ -1,8 +1,5 @@
-import functools
-
 import jax
 import jax.numpy as jnp
-import numpy as np
 from jax import lax
 from jax.experimental import pallas as pl
 from jax.experimental.pallas import tpu as pltpu
@@ -29,26 +26,57 @@
 OBS_GROUPS = [[number(a, (t // 2) ^ a, t % 2) for t in range(MEMBERS)] for a in range(NA)]
 
 
-def position_order():
-    row = np.arange(CLUSTERS)
+def order_of(row):
     b, q, r, c = row >> 5, (row >> 4) & 1, (row >> 1) & 7, row & 1
     return ((r ^ b) * 16 + b * 2 + c) * 2 + q
 
 
-ORDER = position_order()
-
-
-def pack_kernel(coef_ref, ids_ref, send_ref, ordered_ref, out_ref):
-    ids = jnp.concatenate([ids_ref[...].astype(F32), jnp.zeros((CLUSTERS, LANES - 9), F32)], axis=1).T[:MEMBERS]
-    ordered = jnp.dot(ids.astype(BF), ordered_ref[...], preferred_element_type=F32)
+def ordered_matrix():
+    position = lax.broadcasted_iota(jnp.int32, (CLUSTERS, CLUSTERS), 0)
+    row = lax.broadcasted_iota(jnp.int32, (CLUSTERS, CLUSTERS), 1)
+    return jnp.where(position == order_of(row), 1.0, 0.0).astype(BF)
+
+
+def pack_kernel(coef_ref, ids_ref, send_ref, out_ref, all_ref, one_ref, extra_ref, sems):
+    small = [pltpu.make_async_copy(ids_ref, all_ref, sems.at[0]), pltpu.make_async_copy(send_ref, one_ref, sems.at[1])]
+    slices = [
+        pltpu.make_async_copy(
+            coef_ref.at[:, pl.ds(t * LANES, LANES)], out_ref.at[t, pl.ds(0, CLUSTERS), :], sems.at[2 + t]
+        )
+        for t in range(MEMBERS)
+    ]
+    for copy in small + slices:
+        copy.start()
+    sort = ordered_matrix()
+    for copy in small:
+        copy.wait()
+    ids = [all_ref[l].astype(F32) for l in range(9)]
     pad = jnp.zeros((3, CLUSTERS), F32)
-    source = jnp.concatenate([ids[:4], send_ref[...].astype(F32), pad], axis=0)
-    other = jnp.concatenate([ordered[4:8], ids[8:9], pad], axis=0)
+    source = jnp.concatenate(ids[:4] + [one_ref[...].astype(F32), pad], axis=0)
+    ordered = jnp.dot(jnp.concatenate(ids[:8], axis=0).astype(BF), sort, preferred_element_type=F32)
+    other = jnp.concatenate([ordered[4:8], ids[8], pad], axis=0)
     extra = jnp.concatenate([source[:, :LANES], source[:, LANES:], other[:, :LANES], other[:, LANES:]], axis=0)
-    extra = extra.astype(BF)
-    for t in range(MEMBERS):
-        out_ref[t, :CLUSTERS, :] = coef_ref[:, t * LANES : (t + 1) * LANES]
-        out_ref[t, CLUSTERS:, :] = extra
+    extra_ref[...] = extra.astype(BF)
+    below = [
+        pltpu.make_async_copy(
+            extra_ref, out_ref.at[t, pl.ds(CLUSTERS, EXTRA), :], sems.at[2 + MEMBERS + t]
+        )
+        for t in range(MEMBERS)
+    ]
+    for copy in below:
+        copy.start()
+    for copy in below + slices:
+        copy.wait()
+
+
+def unpack_kernel(x_ref, out_ref, sems):
+    copies = [
+        pltpu.make_async_copy(x_ref.at[t], out_ref.at[:, pl.ds(t * LANES, LANES)], sems.at[t]) for t in range(MEMBERS)
+    ]
+    for copy in copies:
+        copy.start()
+    for copy in copies:
+        copy.wait()
 
 
 def turned_weights(block, parts, lows):
@@ -65,15 +93,15 @@
 
 
 def table_kernel(
-    src_ref, mid_ref, obs_ref, perm_ref, ordered_ref, order_ref,
+    src_ref, mid_ref, obs_ref, perm_ref,
     src_perm_ref, obs_perm_ref, src_w_ref, obs_w_ref, mid_w_ref,
 ):
     perm = perm_ref[...].astype(F32)
-    moved = jnp.dot(perm.astype(BF), ordered_ref[...], preferred_element_type=F32)
+    moved = jnp.dot(perm.astype(BF), ordered_matrix(), preferred_element_type=F32)
     turned = jnp.concatenate([perm, moved, jnp.zeros((LANES - 16, CLUSTERS), F32)], axis=0).T
     shape = (CLUSTERS, CLUSTERS)
     count = lax.broadcasted_iota(jnp.int32, shape, 1).astype(F32)
-    order = jnp.broadcast_to(order_ref[...], shape)
+    order = order_of(lax.broadcasted_iota(jnp.int32, shape, 1)).astype(F32)
 
     def match(column, against):
         return jnp.where(jnp.broadcast_to(column, shape) == against, 1.0, 0.0).astype(BF)
@@ -95,18 +123,28 @@
         mid_w_ref[form] = turned_weights(lambda k, p, i: mid_ref[k, i].astype(F32), (0,), lows)
 
 
+def coded(kinds):
+    high = jnp.floor(kinds * 0.25)
+    low = kinds - 4.0 * high
+    second = jnp.floor(low * 0.5)
+    return (high + 1.0 + 8.0 * (low - 2.0 * second)) * (1.0 - 2.0 * second)
+
+
 def spread_kinds(kt_ref, kb_ref, row):
     for m in range(MEMBERS):
         for half in range(2):
             col = m * IDS + 8 * half + row
             kinds = jnp.broadcast_to(kt_ref[:, col : col + 1], (LANES, LANES))
-            high = jnp.floor(kinds * 0.25)
-            low = kinds - 4.0 * high
-            second = jnp.floor(low * 0.5)
-            at = slice(half * LANES, (half + 1) * LANES)
-            kb_ref[0, m, at, :] = high.astype(BF)
-            kb_ref[1, m, at, :] = second.astype(BF)
-            kb_ref[2, m, at, :] = (low - 2.0 * second).astype(BF)
+            kb_ref[m, half * LANES : (half + 1) * LANES, :] = kinds.astype(BF)
+
+
+def high_of(code):
+    size = jnp.maximum(code, -code)
+    return jnp.where(size >= 8.0, size - 8.0, size)
+
+
+def odd_of(code):
+    return jnp.maximum(code, -code) >= 8.0
 
 
 def first_side():
@@ -119,14 +157,14 @@
 
 def expand(x, high):
     zero = jnp.zeros_like(x)
-    return jnp.concatenate([jnp.where(high == float(j), x, zero) for j in range(4)], axis=1)
+    return jnp.concatenate([jnp.where(high == float(j + 1), x, zero) for j in range(4)], axis=1)
 
 
 def expand_halves(x, high, first):
     zero = jnp.zeros_like(x)
     parts = []
     for j in (0, 2):
-        parts.append(jnp.where(first, jnp.where(high == float(j), x, zero), jnp.where(high == float(j + 1), x, zero)))
+        parts.append(jnp.where(first, jnp.where(high == float(j + 1), x, zero), jnp.where(high == float(j + 2), x, zero)))
     return jnp.concatenate(parts, axis=1)
 
 
@@ -136,7 +174,7 @@
         for side in range(2)
     ]
     for k, m in enumerate(ms):
-        second, odd = kb_ref[1, m] > 0.5, kb_ref[2, m] > 0.5
+        second, odd = kb_ref[m] < 0.0, odd_of(kb_ref[m])
         at = slice(k * CLUSTERS, (k + 1) * CLUSTERS)
         one, two = [jnp.where(second, p[at, LANES:].astype(BF), p[at, :LANES].astype(BF)) for p in prods]
         kept = jnp.where(jnp.logical_xor(first, odd), one, two)
@@ -159,7 +197,7 @@
             own = [own[:, k * LANES : (k + 1) * LANES] for k in range(BATCH)]
         rows = []
         for k, m in enumerate(ms):
-            x, y, high = own[k], far[:, k * LANES : (k + 1) * LANES], kb_ref[0, m]
+            x, y, high = own[k], far[:, k * LANES : (k + 1) * LANES], high_of(kb_ref[m])
             rows.append((expand(jnp.where(first, x, y), high), expand(jnp.where(first, y, x), high)))
         multiply(ms, rows, weights, kb_ref, write, first)
         return carry
@@ -169,9 +207,11 @@
 
 def source_kernel(place_ref, x_ref, perm_ref, w_ref, out_ref, kt_ref, kb_ref, s_ref, t_ref, f_ref):
     b = place_ref[0]
-    kt_ref[...] = x_ref[:, CLUSTERS : CLUSTERS + IDS, :].reshape(MEMBERS * IDS, LANES).astype(F32).T
+    ids = x_ref[:, CLUSTERS : CLUSTERS + IDS, :].reshape(MEMBERS * IDS, LANES).astype(F32).T
+    kt_ref[0] = ids
+    kt_ref[1] = coded(ids)
     for l, mask in enumerate((2, 4, 8, 1)):
-        spread_kinds(kt_ref, kb_ref, l)
+        spread_kinds(kt_ref.at[1], kb_ref, l)
 
         def read(m, l=l):
             return x_ref[m, :CLUSTERS, :] if l == 0 else s_ref[(l - 1) % 2, m]
@@ -189,7 +229,7 @@
         picks = []
         for half in range(2):
             col = m * IDS + 8 * half + 4
-            at = jnp.broadcast_to(kt_ref[:, col : col + 1], (LANES, LANES))
+            at = jnp.broadcast_to(kt_ref[0, :, col : col + 1], (LANES, LANES))
             picks.append(
                 jnp.concatenate([(at == lane).astype(F32), (at == lane + LANES).astype(F32)], axis=1).astype(BF)
             )
@@ -210,8 +250,8 @@
 def observation_kernel(place_ref, r_ref, perm_ref, w_ref, wmid_ref, out_ref, kt_ref, kb_ref, s_ref, t_ref):
     b, diag = place_ref[0], place_ref[1]
     ids = [r_ref[(n // 2) ^ b, pl.ds(MEMBERS * EXTRA + (n % 2) * IDS, IDS), :] for n in range(MEMBERS)]
-    kt_ref[...] = jnp.concatenate(ids, axis=0).astype(F32).T
-    spread_kinds(kt_ref, kb_ref, 0)
+    kt_ref[1] = coded(jnp.concatenate(ids, axis=0).astype(F32).T)
+    spread_kinds(kt_ref.at[1], kb_ref, 0)
 
     def put(slot):
         def write(n, value, turned):
@@ -227,7 +267,7 @@
         for n in ns:
             at = pl.ds(pl.multiple_of(n * EXTRA, EXTRA), EXTRA)
             x = jnp.concatenate([r_ref[j ^ diag, at, :] for j in range(NA)], axis=0)
-            turned, high = other_side(x), kb_ref[0, n]
+            turned, high = other_side(x), high_of(kb_ref[n])
             one, two = jnp.where(first, x, turned), jnp.where(first, turned, x)
             rows.append((expand_halves(one, high, first), expand_halves(two, high, first)))
         multiply(ns, rows, wmid_ref, kb_ref, put(1), first)
@@ -235,7 +275,7 @@
 
     lax.fori_loop(0, MEMBERS // BATCH, middle, 0)
     for l, mask in enumerate((8, 4, 2, 1)):
-        spread_kinds(kt_ref, kb_ref, l + 1)
+        spread_kinds(kt_ref.at[1], kb_ref, l + 1)
 
         def read(n, l=l):
             return s_ref[(l + 1) % 2, n]
@@ -252,18 +292,22 @@
 
 VMEM = pl.BlockSpec(memory_space=pltpu.VMEM)
 SMEM = pl.BlockSpec(memory_space=pltpu.SMEM)
-LIMIT = 40 * 1024 * 1024
-
-
-def call(kernel, name, out_shape, in_specs, scratch=(), flops=0, count=0):
+HBM = pl.BlockSpec(memory_space=pltpu.HBM)
+LIMIT = 24 * 1024 * 1024
+TABLES = 16 * 1024 * 1024
+SMALL = 4 * 1024 * 1024
+
+
+def call(kernel, name, out_shape, in_specs, scratch=(), out_spec=None, limit=None, flops=0, count=0):
     many = isinstance(out_shape, tuple)
+    spec = VMEM if out_spec is None else out_spec
     return pl.pallas_call(
         kernel,
         out_shape=out_shape,
         in_specs=in_specs,
-        out_specs=(VMEM,) * len(out_shape) if many else VMEM,
+        out_specs=(spec,) * len(out_shape) if many else spec,
         scratch_shapes=list(scratch),
-        compiler_params=pltpu.CompilerParams(vmem_limit_bytes=LIMIT),
+        compiler_params=pltpu.CompilerParams(vmem_limit_bytes=LIMIT if limit is None else limit),
         cost_estimate=pl.CostEstimate(flops=flops, bytes_accessed=count, transcendentals=0),
         name=name,
     )
@@ -273,29 +317,40 @@
     a = lax.axis_index("gx")
     b = lax.axis_index("gy") // 2
     place = jnp.stack([b, a ^ b]).astype(jnp.int32)
-    ordered = jnp.asarray(np.eye(CLUSTERS)[:, ORDER], BF)
-    order = jnp.asarray(ORDER[None], F32)
 
     def shape(*dims):
         return jax.ShapeDtypeStruct(dims, BF)
 
-    x = call(pack_kernel, "pack", shape(MEMBERS, CLUSTERS + EXTRA, LANES), [VMEM] * 4, count=2**21)(
-        coefficients[0, 0], block_ids[0, 0], owner_order[0], ordered
-    )
+    x = call(
+        pack_kernel,
+        "pack",
+        shape(MEMBERS, CLUSTERS + EXTRA, LANES),
+        [HBM] * 3,
+        (
+            pltpu.VMEM((9, 1, CLUSTERS), jnp.int32),
+            pltpu.VMEM((1, CLUSTERS), jnp.int32),
+            pltpu.VMEM((EXTRA, LANES), BF),
+            pltpu.SemaphoreType.DMA((2 + 2 * MEMBERS,)),
+        ),
+        out_spec=HBM,
+        limit=SMALL,
+        count=2**21,
+    )(coefficients[0, 0], block_ids[0, 0].T[:, None, :], owner_order[0])
     x = lax.all_to_all(x, AXES, split_axis=0, concat_axis=0, tiled=True, axis_index_groups=SRC_GROUPS)
     square, wide = (CLUSTERS, CLUSTERS), (2, 8 * HALF, 4 * HALF)
     src_perm, obs_perm, src_w, obs_w, mid_w = call(
         table_kernel,
         "tables",
         (shape(4, *square), shape(5, *square), shape(4, *wide), shape(4, *wide), shape(2, 4 * HALF, 4 * HALF)),
-        [VMEM] * 6,
+        [VMEM] * 4,
+        limit=TABLES,
         flops=10**9,
         count=2**24,
-    )(src_blocks, mid_blocks, obs_blocks, partner_perm, ordered, order)
-
-    ids = pltpu.VMEM((LANES, MEMBERS * IDS), F32)
+    )(src_blocks, mid_blocks, obs_blocks, partner_perm)
+
+    ids = pltpu.VMEM((2, LANES, MEMBERS * IDS), F32)
+    kinds = pltpu.VMEM((MEMBERS, CLUSTERS, LANES), BF)
     state = pltpu.VMEM((2, MEMBERS, CLUSTERS, LANES), BF)
-    kinds = pltpu.VMEM((3, MEMBERS, CLUSTERS, LANES), BF)
     mid = call(
         source_kernel,
         "source_levels",
@@ -311,14 +366,17 @@
         [SMEM, VMEM, VMEM, VMEM, VMEM],
         (ids, kinds, state, state),
     )(place, mid, obs_perm, obs_w, mid_w)
-    out = lax.all_to_all(
-        done.reshape(MEMBERS * CLUSTERS, LANES),
-        AXES,
-        split_axis=0,
-        concat_axis=1,
-        tiled=True,
-        axis_index_groups=OBS_GROUPS,
-    )
+    out = lax.all_to_all(done, AXES, split_axis=0, concat_axis=0, tiled=True, axis_index_groups=OBS_GROUPS)
+    out = call(
+        unpack_kernel,
+        "unpack",
+        shape(CLUSTERS, MEMBERS * LANES),
+        [pl.BlockSpec(memory_space=pl.ANY)],
+        (pltpu.SemaphoreType.DMA((MEMBERS,)),),
+        out_spec=HBM,
+        limit=SMALL,
+        count=2**21,
+    )(out)
     return out.reshape(1, 1, CLUSTERS, MEMBERS * LANES)
 
 

time: 127 us -> 122 us (0.961)
  local copies, waits for them, and re-layouts: 15.7 us -> 10.5 us
    unnamed x39 -> x29, local copies, waits for them, and re-layouts: 13.8 us -> 10.5 us
    reshape x1 -> x0, local copies, waits for them, and re-layouts: 1.42 us -> none  [on_device(): return out.reshape(1, 1, CLUSTERS, MEMBERS * LANES)]
where the time goes in v2:
time: 122 us; the launch traced here: 121 us
  Pallas kernels  50.8 us (42%)
  blocking collectives  48.3 us (40%)
  local copies, waits for them, and re-layouts  10.5 us (9%)
  starting transfers between devices  6.93 us (6%)
  waiting for transfers between devices  4.47 us (4%)
    all_to_all x1, blocking collectives, on_device(): lax.all_to_all(mid, AXES, split_axis=0, concat_axis=0, tiled=True, axis_i...  26.3 us
    pallas_call x1, Pallas kernels, on_device(): call(observation_kernel, 'observation_levels', shape(MEMBERS, CLUSTERS, L...  22 us
    all_to_all x1, blocking collectives, on_device(): lax.all_to_all(done, AXES, split_axis=0, concat_axis=0, tiled=True, axis_...  22 us
    pallas_call x1, Pallas kernels, on_device(): call(source_kernel, 'source_levels', shape(NA, (MEMBERS + 1) * EXTRA, LAN...  20.5 us
    unnamed x29, local copies, waits for them, and re-layouts  10.5 us
    all_to_all x1, starting transfers between devices, on_device(): lax.all_to_all(x, AXES, split_axis=0, concat_axis=0, tiled=True, axis_ind...  6.93 us
    pallas_call x1, Pallas kernels, on_device(): call(table_kernel, 'tables', (shape(4, *square), shape(5, *square), shape...  5.88 us
    all_to_all x1, waiting for transfers between devices, on_device(): lax.all_to_all(x, AXES, split_axis=0, concat_axis=0, tiled=True, axis_ind...  4.47 us
  transfers between devices with their start and end apart: 1, of which 1 were waited for; matrix products, arithmetic and copies ran while one was open for 0% of the time, Pallas kernels for 5%

profile of v2, /device:TPU:1, one launch (start us, length us, event | category | flops | bytes accessed | tf_op | source)
XLA Modules:
  0.0 121.3 jit_solution(15372514212543651716)
XLA Ops:
  0.0 0.7 copy.10
  0.7 0.0 copy-start.4
  0.7 1.2 %copy-done.4 = bf16[1,1,256,2048]{3,2,1,0:T(8,128)(2,1)S(1)} copy-done((bf16[1,1,256,2048]{3,2,1,0:T(8,128)(2,1)S(1)}, bf16[1,1,256,2048]{3,2,1,0:T(8,128)(2,1)}, u32[]{:S(2)}) %copy-start.4) | copy-done | bytes 1048600
  1.9 0.0 copy-start.13
  1.9 0.7 copy-done.13
  2.6 0.0 copy-start.9
  2.6 0.0 copy-start.12
  2.6 1.4 %pack.1 = bf16[16,288,128]{2,1,0:T(8,128)(2,1)} custom-call(bf16[256,2048]{1,0:T(8,128)(2,1)S(1)} %bitcast.10, s32[9,1,256]{2,1,0:T(1,128)S(1)} %broadcast_in_dim.3.ids_ref, s32[1,256]{1,0:T(1,128)S(1)} %bitcast.11), custom_call_target="tpu_custom_call" | custom-call | bytes 2097152 | tf_op jit(solution)/shard_map/pack/pallas_call | solution.py:324
  4.0 6.9 %all-to-all-start = ((bf16[16,288,128]{2,1,0:T(8,128)(2,1)}), bf16[16,288,128]{2,1,0:T(8,128)(2,1)S(1)}, u32[]{:S(2)}, u32[]{:S(2)}) async-start(bf16[16,288,128]{2,1,0:T(8,128)(2,1)} %pack.1), calls=%async_computation | async-start | bytes 2359296 | tf_op jit(solution)/shard_map/all_to_all | solution.py:339
  10.9 0.0 copy-done.9
  10.9 0.0 copy-done.12
  10.9 0.0 copy-start
  11.0 1.6 %copy-done = bf16[4,16,2,2,32,32]{5,4,3,2,1,0:T(8,128)(2,1)S(1)} copy-done((bf16[4,16,2,2,32,32]{5,4,3,2,1,0:T(8,128)(2,1)S(1)}, bf16[4,16,2,2,32,32]{5,4,3,2,1,0:T(8,128)(2,1)}, u32[]{:S(2)}) %copy-start) | copy-done | bytes 524312
  12.5 0.0 copy-start.1
  12.5 1.6 %copy-done.1 = bf16[4,16,2,2,32,32]{5,4,3,2,1,0:T(8,128)(2,1)S(1)} copy-done((bf16[4,16,2,2,32,32]{5,4,3,2,1,0:T(8,128)(2,1)S(1)}, bf16[4,16,2,2,32,32]{5,4,3,2,1,0:T(8,128)(2,1)}, u32[]{:S(2)}) %copy-start.1) | copy-done | bytes 524312
  14.1 5.9 %tables.1 = (bf16[4,256,256]{2,1,0:T(8,128)(2,1)S(1)}, bf16[5,256,256]{2,1,0:T(8,128)(2,1)S(1)}, bf16[4,2,512,256]{3,2,1,0:T(8,128)(2,1)S(1)}, bf16[4,2,512,256]...) custom-call(bf16[4,16,2,2,32,32]{5,4,3,2,1,0:T(8,128)(2,1)S(1)} %copy-done, bf16[16,2,32,32]{3,2,1,0:T(8,128)(2,1)S(1)} %copy-done.9, ...), custom_call_target="tpu_custom_call" | custom-call | flops 1000000000 | bytes 16777216 | tf_op jit(solution)/shard_map/tables/pallas_call | solution.py:341
  20.0 0.0 copy-start.2
  20.0 1.3 %copy-done.2 = bf16[4,2,512,256]{3,2,1,0:T(8,128)(2,1)} copy-done((bf16[4,2,512,256]{3,2,1,0:T(8,128)(2,1)}, bf16[4,2,512,256]{3,2,1,0:T(8,128)(2,1)S(1)}, u32[]{:S(2)}) %copy-start.2) | copy-done | bytes 2097176
  21.3 0.0 copy-start.5
  21.3 0.8 copy-done.5
  22.2 0.0 copy-start.7
  22.2 0.8 copy-done.7
  23.0 0.0 copy-start.10
  23.0 0.7 copy-done.10
  23.7 0.1 pad_add_fusion.place_ref
  23.7 4.5 %all-to-all-done.x_ref = bf16[16,288,128]{2,1,0:T(8,128)(2,1)S(1)} async-done(((bf16[16,288,128]{2,1,0:T(8,128)(2,1)}), bf16[16,288,128]{2,1,0:T(8,128)(2,1)S(1)}, u32[]{:S(2)}, u32[]{:S(2)}) %all-to-all-start) | async-done | bytes 1179680 | tf_op jit(solution)/shard_map/all_to_all | solution.py:339
  28.2 0.0 copy-start.8
  28.2 1.0 copy-done.8
  29.3 0.0 copy-start.6
  29.3 0.0 copy-start.11
  29.3 20.5 %source_levels.1 = bf16[8,544,128]{2,1,0:T(8,128)(2,1)S(1)} custom-call(s32[2]{0:T(128)S(1)} %pad_add_fusion.place_ref, bf16[16,288,128]{2,1,0:T(8,128)(2,1)S(1)} %all-to-all-done.x_ref, bf16[4,256,256]{2,1,0:T(8,128)(2,1)S(1)} %copy-done.8, bf16[4,2,512,256]{3,2,1,0:T(8,128)(2,1)S(1)} %get-tuple-element.11.w_ref), custom_call_target="tpu_custom_call" | custom-call | tf_op jit(solution)/shard_map/source_levels/pallas_call | solution.py:354
  49.7 0.0 copy-start.3
  49.7 26.3 %all_to_all.15.r_ref = bf16[8,544,128]{2,1,0:T(8,128)(2,1)S(1)} all-to-all(bf16[8,544,128]{2,1,0:T(8,128)(2,1)S(1)} %source_levels.1), channel_id=1, replica_groups={{0,18,36,54,72,90,108,126},{1,19,37,55,73,91,109,127},{2,16,38,52,74,88..., dimensions={0} | all-to-all | bytes 2228224 | tf_op jit(solution)/shard_map/all_to_all | solution.py:361
  76.0 0.0 copy-done.6
  76.0 0.0 copy-done.11
  76.0 0.0 copy-done.3
  76.0 22.0 %observation_levels.1 = bf16[16,256,128]{2,1,0:T(8,128)(2,1)S(1)} custom-call(s32[2]{0:T(128)S(1)} %pad_add_fusion.place_ref, bf16[8,544,128]{2,1,0:T(8,128)(2,1)S(1)} %all_to_all.15.r_ref, bf16[5,256,256]{2,1,0:T(8,128)(2,1)S(1)} %copy-done.6, bf16[4,2,512,256]{3,2,1,0:T(8,128)(2,1)S(1)} %copy-done.3, bf16[2,256,256]{2,1,0:T(8,128)(2,1)S(1)} %copy-done.11), custom_call_target="tpu_custom_call" | custom-call | tf_op jit(solution)/shard_map/observation_levels/pallas_call | solution.py:362
  98.1 22.0 %all_to_all.16.x_ref = bf16[16,256,128]{2,1,0:T(8,128)(2,1)S(1)} all-to-all(bf16[16,256,128]{2,1,0:T(8,128)(2,1)S(1)} %observation_levels.1), channel_id=1, replica_groups={{0,1,2,3,4,5,6,7,8,9,10,11,12,13,14,15},{18,19,16,17,22,23,20,21,26,27,..., dimensions={0} | all-to-all | bytes 2097152 | tf_op jit(solution)/shard_map/all_to_all | solution.py:369
  120.1 1.1 unpack.1
  (1 shorter events, 0.0 us)
Async XLA Ops:
  0.7 1.2 %copy-start.4 = (bf16[1,1,256,2048]{3,2,1,0:T(8,128)(2,1)S(1)}, bf16[1,1,256,2048]{3,2,1,0:T(8,128)(2,1)}, u32[]{:S(2)}) copy-start(bf16[1,1,256,2048]{3,2,1,0:T(8,128)(2,1)} %param.7) | copy-start | bytes 3145732
  1.9 0.7 copy-start.13
  2.6 8.3 %copy-start.9 = (bf16[16,2,32,32]{3,2,1,0:T(8,128)(2,1)S(1)}, bf16[16,2,32,32]{3,2,1,0:T(8,128)(2,1)}, u32[]{:S(2)}) copy-start(bf16[16,2,32,32]{3,2,1,0:T(8,128)(2,1)} %mid_ref.1) | copy-start | bytes 196612
  2.6 8.3 %copy-start.12 = (s32[8,256]{1,0:T(8,128)S(1)}, s32[8,256]{1,0:T(8,128)}, u32[]{:S(2)}) copy-start(s32[8,256]{1,0:T(8,128)} %perm_ref.1) | copy-start | bytes 24580
  4.0 24.2 %all-to-all-start = ((bf16[16,288,128]{2,1,0:T(8,128)(2,1)}), bf16[16,288,128]{2,1,0:T(8,128)(2,1)S(1)}, u32[]{:S(2)}, u32[]{:S(2)}) async-start(bf16[16,288,128]{2,1,0:T(8,128)(2,1)} %pack.1), calls=%async_computation | async-start | bytes 2359296 | tf_op jit(solution)/shard_map/all_to_all | solution.py:339
  10.9 1.6 %copy-start = (bf16[4,16,2,2,32,32]{5,4,3,2,1,0:T(8,128)(2,1)S(1)}, bf16[4,16,2,2,32,32]{5,4,3,2,1,0:T(8,128)(2,1)}, u32[]{:S(2)}) copy-start(bf16[4,16,2,2,32,32]{5,4,3,2,1,0:T(8,128)(2,1)} %src_ref.1) | copy-start | bytes 1572868
  12.5 1.6 %copy-start.1 = (bf16[4,16,2,2,32,32]{5,4,3,2,1,0:T(8,128)(2,1)S(1)}, bf16[4,16,2,2,32,32]{5,4,3,2,1,0:T(8,128)(2,1)}, u32[]{:S(2)}) copy-start(bf16[4,16,2,2,32,32]{5,4,3,2,1,0:T(8,128)(2,1)} %obs_ref.1) | copy-start | bytes 1572868
  20.0 1.3 %copy-start.2 = (bf16[4,2,512,256]{3,2,1,0:T(8,128)(2,1)}, bf16[4,2,512,256]{3,2,1,0:T(8,128)(2,1)S(1)}, u32[]{:S(2)}) copy-start(bf16[4,2,512,256]{3,2,1,0:T(8,128)(2,1)S(1)} %get-tuple-element.13.w_ref) | copy-start | bytes 6291460
  21.3 0.8 copy-start.5
  22.2 0.8 copy-start.7
  23.0 0.7 copy-start.10
  28.2 1.0 copy-start.8
  29.3 46.8 %copy-start.6 = (bf16[5,256,256]{2,1,0:T(8,128)(2,1)S(1)}, bf16[5,256,256]{2,1,0:T(8,128)(2,1)}, u32[]{:S(2)}) copy-start(bf16[5,256,256]{2,1,0:T(8,128)(2,1)} %copy-done.5) | copy-start | bytes 1966084
  29.3 46.8 %copy-start.11 = (bf16[2,256,256]{2,1,0:T(8,128)(2,1)S(1)}, bf16[2,256,256]{2,1,0:T(8,128)(2,1)}, u32[]{:S(2)}) copy-start(bf16[2,256,256]{2,1,0:T(8,128)(2,1)} %copy-done.10) | copy-start | bytes 786436
  49.7 26.3 %copy-start.3 = (bf16[4,2,512,256]{3,2,1,0:T(8,128)(2,1)S(1)}, bf16[4,2,512,256]{3,2,1,0:T(8,128)(2,1)}, u32[]{:S(2)}) copy-start(bf16[4,2,512,256]{3,2,1,0:T(8,128)(2,1)} %copy-done.2) | copy-start | bytes 6291460

commit v3 on v2

--- a/solution.py
+++ b/solution.py
@@ -135,7 +135,7 @@
         for half in range(2):
             col = m * IDS + 8 * half + row
             kinds = jnp.broadcast_to(kt_ref[:, col : col + 1], (LANES, LANES))
-            kb_ref[m, half * LANES : (half + 1) * LANES, :] = kinds.astype(BF)
+            kb_ref[m, half * LANES : (half + 1) * LANES, :] = kinds
 
 
 def high_of(code):
@@ -169,20 +169,23 @@
 
 
 def multiply(ms, rows, weights, kb_ref, write, first):
-    prods = [
-        jnp.dot(jnp.concatenate([r[side] for r in rows], axis=0), weights[side], preferred_element_type=F32)
-        for side in range(2)
-    ]
+    kept_sides = []
+    for side in range(2):
+        prod = jnp.dot(jnp.concatenate([r[side]() for r in rows], axis=0), weights[side], preferred_element_type=F32)
+        each = []
+        for k, m in enumerate(ms):
+            at = slice(k * CLUSTERS, (k + 1) * CLUSTERS)
+            each.append(jnp.where(kb_ref[m] < 0.0, prod[at, LANES:], prod[at, :LANES]).astype(BF))
+        kept_sides.append(each)
     for k, m in enumerate(ms):
-        second, odd = kb_ref[m] < 0.0, odd_of(kb_ref[m])
-        at = slice(k * CLUSTERS, (k + 1) * CLUSTERS)
-        one, two = [jnp.where(second, p[at, LANES:].astype(BF), p[at, :LANES].astype(BF)) for p in prods]
+        odd = odd_of(kb_ref[m].astype(BF))
+        one, two = kept_sides[0][k], kept_sides[1][k]
         kept = jnp.where(jnp.logical_xor(first, odd), one, two)
         turned = other_side(kept)
         write(m, jnp.where(odd, turned, kept), jnp.where(odd, kept, turned))
 
 
-BATCH = 8
+BATCH = 16
 
 
 def level(read, read_turned, write, perm, weights, kb_ref, mask, own_perm=None):
@@ -197,8 +200,8 @@
             own = [own[:, k * LANES : (k + 1) * LANES] for k in range(BATCH)]
         rows = []
         for k, m in enumerate(ms):
-            x, y, high = own[k], far[:, k * LANES : (k + 1) * LANES], high_of(kb_ref[m])
-            rows.append((expand(jnp.where(first, x, y), high), expand(jnp.where(first, y, x), high)))
+            x, y, high = own[k], far[:, k * LANES : (k + 1) * LANES], high_of(kb_ref[m].astype(BF))
+            rows.append((lambda x=x, y=y, high=high: expand(jnp.where(first, x, y), high), lambda x=x, y=y, high=high: expand(jnp.where(first, y, x), high)))
         multiply(ms, rows, weights, kb_ref, write, first)
         return carry
 
@@ -267,9 +270,9 @@
         for n in ns:
             at = pl.ds(pl.multiple_of(n * EXTRA, EXTRA), EXTRA)
             x = jnp.concatenate([r_ref[j ^ diag, at, :] for j in range(NA)], axis=0)
-            turned, high = other_side(x), high_of(kb_ref[n])
+            turned, high = other_side(x), high_of(kb_ref[n].astype(BF))
             one, two = jnp.where(first, x, turned), jnp.where(first, turned, x)
-            rows.append((expand_halves(one, high, first), expand_halves(two, high, first)))
+            rows.append((lambda one=one, high=high: expand_halves(one, high, first), lambda two=two, high=high: expand_halves(two, high, first)))
         multiply(ns, rows, wmid_ref, kb_ref, put(1), first)
         return carry
 
@@ -335,7 +338,7 @@
         out_spec=HBM,
         limit=SMALL,
         count=2**21,
-    )(coefficients[0, 0], block_ids[0, 0].T[:, None, :], owner_order[0])
+    )(coefficients[0, 0], lax.transpose(block_ids, (0, 3, 1, 2))[0], owner_order[0])
     x = lax.all_to_all(x, AXES, split_axis=0, concat_axis=0, tiled=True, axis_index_groups=SRC_GROUPS)
     square, wide = (CLUSTERS, CLUSTERS), (2, 8 * HALF, 4 * HALF)
     src_perm, obs_perm, src_w, obs_w, mid_w = call(
@@ -349,7 +352,7 @@
     )(src_blocks, mid_blocks, obs_blocks, partner_perm)
 
     ids = pltpu.VMEM((2, LANES, MEMBERS * IDS), F32)
-    kinds = pltpu.VMEM((MEMBERS, CLUSTERS, LANES), BF)
+    kinds = pltpu.VMEM((MEMBERS, CLUSTERS, LANES), F32)
     state = pltpu.VMEM((2, MEMBERS, CLUSTERS, LANES), BF)
     mid = call(
         source_kernel,

time: 122 us -> 107 us (0.88)
  Pallas kernels: 50.8 us -> 36.3 us
    pallas_call x1, Pallas kernels: 22 us -> 14.1 us  [on_device(): call(observation_kernel, 'observation_levels', shape(MEMBERS, CLUSTERS, L...]
    pallas_call x1, Pallas kernels: 20.5 us -> 13.9 us  [on_device(): call(source_kernel, 'source_levels', shape(NA, (MEMBERS + 1) * EXTRA, LAN...]
    unnamed x29 -> x30, local copies, waits for them, and re-layouts: 10.5 us -> 10.5 us
  transfers between devices with their start and end apart: 1 -> 1, of which waited for: 1 -> 1; matrix products, arithmetic and copies ran while one was open for 0% -> 0% of each run, Pallas kernels for 5% -> 6%
where the time goes in v3:
time: 107 us
  blocking collectives  48.3 us (45%)
  Pallas kernels  36.3 us (34%)
  local copies, waits for them, and re-layouts  10.5 us (10%)
  starting transfers between devices  6.93 us (6%)
  waiting for transfers between devices  4.48 us (4%)
    all_to_all x1, blocking collectives, on_device(): lax.all_to_all(mid, AXES, split_axis=0, concat_axis=0, tiled=True, axis_i...  26.3 us
    all_to_all x1, blocking collectives, on_device(): lax.all_to_all(done, AXES, split_axis=0, concat_axis=0, tiled=True, axis_...  22 us
    pallas_call x1, Pallas kernels, on_device(): call(observation_kernel, 'observation_levels', shape(MEMBERS, CLUSTERS, L...  14.1 us
    pallas_call x1, Pallas kernels, on_device(): call(source_kernel, 'source_levels', shape(NA, (MEMBERS + 1) * EXTRA, LAN...  13.9 us
    unnamed x30, local copies, waits for them, and re-layouts  10.5 us
    all_to_all x1, starting transfers between devices, on_device(): lax.all_to_all(x, AXES, split_axis=0, concat_axis=0, tiled=True, axis_ind...  6.93 us
    pallas_call x1, Pallas kernels, on_device(): call(table_kernel, 'tables', (shape(4, *square), shape(5, *square), shape...  5.88 us
    all_to_all x1, waiting for transfers between devices, on_device(): lax.all_to_all(x, AXES, split_axis=0, concat_axis=0, tiled=True, axis_ind...  4.48 us
  transfers between devices with their start and end apart: 1, of which 1 were waited for; matrix products, arithmetic and copies ran while one was open for 0% of the time, Pallas kernels for 6%

profile of v3, /device:TPU:1, one launch (start us, length us, event | category | flops | bytes accessed | tf_op | source)
XLA Modules:
  0.0 106.8 jit_solution(1742109982163110469)
XLA Ops:
  0.0 0.0 copy-start.4
  0.0 1.2 %copy-done.4 = bf16[1,1,256,2048]{3,2,1,0:T(8,128)(2,1)S(1)} copy-done((bf16[1,1,256,2048]{3,2,1,0:T(8,128)(2,1)S(1)}, bf16[1,1,256,2048]{3,2,1,0:T(8,128)(2,1)}, u32[]{:S(2)}) %copy-start.4) | copy-done | bytes 1048600
  1.2 0.0 copy-start.12
  1.2 0.7 copy-done.12
  1.9 0.0 copy-start.14
  1.9 0.7 copy-done.14
  2.6 0.0 copy-start.9
  2.6 0.0 copy-start.13
  2.6 1.4 %pack.1 = bf16[16,288,128]{2,1,0:T(8,128)(2,1)} custom-call(bf16[256,2048]{1,0:T(8,128)(2,1)S(1)} %bitcast.8, s32[9,1,256]{2,1,0:T(1,128)S(1)} %bitcast.9, s32[1,256]{1,0:T(1,128)S(1)} %bitcast.10), custom_call_target="tpu_custom_call" | custom-call | bytes 2097152 | tf_op jit(solution)/shard_map/pack/pallas_call | solution.py:327
  4.0 6.9 %all-to-all-start = ((bf16[16,288,128]{2,1,0:T(8,128)(2,1)}), bf16[16,288,128]{2,1,0:T(8,128)(2,1)S(1)}, u32[]{:S(2)}, u32[]{:S(2)}) async-start(bf16[16,288,128]{2,1,0:T(8,128)(2,1)} %pack.1), calls=%async_computation | async-start | bytes 2359296 | tf_op jit(solution)/shard_map/all_to_all | solution.py:342
  10.9 0.0 copy-done.9
  11.0 0.0 copy-done.13
  11.0 0.0 copy-start
  11.0 1.6 %copy-done = bf16[4,16,2,2,32,32]{5,4,3,2,1,0:T(8,128)(2,1)S(1)} copy-done((bf16[4,16,2,2,32,32]{5,4,3,2,1,0:T(8,128)(2,1)S(1)}, bf16[4,16,2,2,32,32]{5,4,3,2,1,0:T(8,128)(2,1)}, u32[]{:S(2)}) %copy-start) | copy-done | bytes 524312
  12.6 0.0 copy-start.1
  12.6 1.6 %copy-done.1 = bf16[4,16,2,2,32,32]{5,4,3,2,1,0:T(8,128)(2,1)S(1)} copy-done((bf16[4,16,2,2,32,32]{5,4,3,2,1,0:T(8,128)(2,1)S(1)}, bf16[4,16,2,2,32,32]{5,4,3,2,1,0:T(8,128)(2,1)}, u32[]{:S(2)}) %copy-start.1) | copy-done | bytes 524312
  14.1 5.9 %tables.1 = (bf16[4,256,256]{2,1,0:T(8,128)(2,1)S(1)}, bf16[5,256,256]{2,1,0:T(8,128)(2,1)S(1)}, bf16[4,2,512,256]{3,2,1,0:T(8,128)(2,1)S(1)}, bf16[4,2,512,256]...) custom-call(bf16[4,16,2,2,32,32]{5,4,3,2,1,0:T(8,128)(2,1)S(1)} %copy-done, bf16[16,2,32,32]{3,2,1,0:T(8,128)(2,1)S(1)} %copy-done.9, ...), custom_call_target="tpu_custom_call" | custom-call | flops 1000000000 | bytes 16777216 | tf_op jit(solution)/shard_map/tables/pallas_call | solution.py:344
  20.0 0.0 copy-start.2
  20.0 1.3 %copy-done.2 = bf16[4,2,512,256]{3,2,1,0:T(8,128)(2,1)} copy-done((bf16[4,2,512,256]{3,2,1,0:T(8,128)(2,1)}, bf16[4,2,512,256]{3,2,1,0:T(8,128)(2,1)S(1)}, u32[]{:S(2)}) %copy-start.2) | copy-done | bytes 2097176
  21.4 0.0 copy-start.5
  21.4 0.8 copy-done.5
  22.2 0.0 copy-start.7
  22.2 0.8 copy-done.7
  23.0 0.0 copy-start.10
  23.0 0.7 copy-done.10
  23.7 0.1 pad_add_fusion.place_ref
  23.8 4.5 %all-to-all-done.x_ref = bf16[16,288,128]{2,1,0:T(8,128)(2,1)S(1)} async-done(((bf16[16,288,128]{2,1,0:T(8,128)(2,1)}), bf16[16,288,128]{2,1,0:T(8,128)(2,1)S(1)}, u32[]{:S(2)}, u32[]{:S(2)}) %all-to-all-start) | async-done | bytes 1179680 | tf_op jit(solution)/shard_map/all_to_all | solution.py:342
  28.2 0.0 copy-start.8
  28.2 1.0 copy-done.8
  29.3 0.0 copy-start.6
  29.3 0.0 copy-start.11
  29.3 13.9 %source_levels.1 = bf16[8,544,128]{2,1,0:T(8,128)(2,1)S(1)} custom-call(s32[2]{0:T(128)S(1)} %pad_add_fusion.place_ref, bf16[16,288,128]{2,1,0:T(8,128)(2,1)S(1)} %all-to-all-done.x_ref, bf16[4,256,256]{2,1,0:T(8,128)(2,1)S(1)} %copy-done.8, bf16[4,2,512,256]{3,2,1,0:T(8,128)(2,1)S(1)} %get-tuple-element.11.w_ref), custom_call_target="tpu_custom_call" | custom-call | tf_op jit(solution)/shard_map/source_levels/pallas_call | solution.py:357
  43.1 0.0 copy-start.3
  43.2 26.3 %all_to_all.15.r_ref = bf16[8,544,128]{2,1,0:T(8,128)(2,1)S(1)} all-to-all(bf16[8,544,128]{2,1,0:T(8,128)(2,1)S(1)} %source_levels.1), channel_id=1, replica_groups={{0,18,36,54,72,90,108,126},{1,19,37,55,73,91,109,127},{2,16,38,52,74,88..., dimensions={0} | all-to-all | bytes 2228224 | tf_op jit(solution)/shard_map/all_to_all | solution.py:364
  69.5 0.0 copy-done.6
  69.5 0.0 copy-done.11
  69.5 0.0 copy-done.3
  69.5 14.1 %observation_levels.1 = bf16[16,256,128]{2,1,0:T(8,128)(2,1)S(1)} custom-call(s32[2]{0:T(128)S(1)} %pad_add_fusion.place_ref, bf16[8,544,128]{2,1,0:T(8,128)(2,1)S(1)} %all_to_all.15.r_ref, bf16[5,256,256]{2,1,0:T(8,128)(2,1)S(1)} %copy-done.6, bf16[4,2,512,256]{3,2,1,0:T(8,128)(2,1)S(1)} %copy-done.3, bf16[2,256,256]{2,1,0:T(8,128)(2,1)S(1)} %copy-done.11), custom_call_target="tpu_custom_call" | custom-call | tf_op jit(solution)/shard_map/observation_levels/pallas_call | solution.py:365
  83.5 22.0 %all_to_all.16.x_ref = bf16[16,256,128]{2,1,0:T(8,128)(2,1)S(1)} all-to-all(bf16[16,256,128]{2,1,0:T(8,128)(2,1)S(1)} %observation_levels.1), channel_id=1, replica_groups={{0,1,2,3,4,5,6,7,8,9,10,11,12,13,14,15},{18,19,16,17,22,23,20,21,26,27,..., dimensions={0} | all-to-all | bytes 2097152 | tf_op jit(solution)/shard_map/all_to_all | solution.py:372
  105.5 1.1 %unpack.1 = bf16[256,2048]{1,0:T(8,128)(2,1)} custom-call(bf16[16,256,128]{2,1,0:T(8,128)(2,1)S(1)} %all_to_all.16.x_ref), custom_call_target="tpu_custom_call" | custom-call | bytes 2097152 | tf_op jit(solution)/shard_map/unpack/pallas_call | solution.py:373
Async XLA Ops:
  0.0 1.2 %copy-start.4 = (bf16[1,1,256,2048]{3,2,1,0:T(8,128)(2,1)S(1)}, bf16[1,1,256,2048]{3,2,1,0:T(8,128)(2,1)}, u32[]{:S(2)}) copy-start(bf16[1,1,256,2048]{3,2,1,0:T(8,128)(2,1)} %param.7) | copy-start | bytes 3145732
  1.2 0.7 copy-start.12
  1.9 0.7 copy-start.14
  2.6 8.3 %copy-start.9 = (bf16[16,2,32,32]{3,2,1,0:T(8,128)(2,1)S(1)}, bf16[16,2,32,32]{3,2,1,0:T(8,128)(2,1)}, u32[]{:S(2)}) copy-start(bf16[16,2,32,32]{3,2,1,0:T(8,128)(2,1)} %mid_ref.1) | copy-start | bytes 196612
  2.6 8.3 %copy-start.13 = (s32[8,256]{1,0:T(8,128)S(1)}, s32[8,256]{1,0:T(8,128)}, u32[]{:S(2)}) copy-start(s32[8,256]{1,0:T(8,128)} %perm_ref.1) | copy-start | bytes 24580
  4.0 24.2 %all-to-all-start = ((bf16[16,288,128]{2,1,0:T(8,128)(2,1)}), bf16[16,288,128]{2,1,0:T(8,128)(2,1)S(1)}, u32[]{:S(2)}, u32[]{:S(2)}) async-start(bf16[16,288,128]{2,1,0:T(8,128)(2,1)} %pack.1), calls=%async_computation | async-start | bytes 2359296 | tf_op jit(solution)/shard_map/all_to_all | solution.py:342
  11.0 1.6 %copy-start = (bf16[4,16,2,2,32,32]{5,4,3,2,1,0:T(8,128)(2,1)S(1)}, bf16[4,16,2,2,32,32]{5,4,3,2,1,0:T(8,128)(2,1)}, u32[]{:S(2)}) copy-start(bf16[4,16,2,2,32,32]{5,4,3,2,1,0:T(8,128)(2,1)} %src_ref.1) | copy-start | bytes 1572868
  12.6 1.6 %copy-start.1 = (bf16[4,16,2,2,32,32]{5,4,3,2,1,0:T(8,128)(2,1)S(1)}, bf16[4,16,2,2,32,32]{5,4,3,2,1,0:T(8,128)(2,1)}, u32[]{:S(2)}) copy-start(bf16[4,16,2,2,32,32]{5,4,3,2,1,0:T(8,128)(2,1)} %obs_ref.1) | copy-start | bytes 1572868
  20.0 1.3 %copy-start.2 = (bf16[4,2,512,256]{3,2,1,0:T(8,128)(2,1)}, bf16[4,2,512,256]{3,2,1,0:T(8,128)(2,1)S(1)}, u32[]{:S(2)}) copy-start(bf16[4,2,512,256]{3,2,1,0:T(8,128)(2,1)S(1)} %get-tuple-element.13.w_ref) | copy-start | bytes 6291460
  21.4 0.8 copy-start.5
  22.2 0.8 copy-start.7
  23.0 0.7 copy-start.10
  28.2 1.0 copy-start.8
  29.3 40.2 %copy-start.6 = (bf16[5,256,256]{2,1,0:T(8,128)(2,1)S(1)}, bf16[5,256,256]{2,1,0:T(8,128)(2,1)}, u32[]{:S(2)}) copy-start(bf16[5,256,256]{2,1,0:T(8,128)(2,1)} %copy-done.5) | copy-start | bytes 1966084
  29.3 40.2 %copy-start.11 = (bf16[2,256,256]{2,1,0:T(8,128)(2,1)S(1)}, bf16[2,256,256]{2,1,0:T(8,128)(2,1)}, u32[]{:S(2)}) copy-start(bf16[2,256,256]{2,1,0:T(8,128)(2,1)} %copy-done.10) | copy-start | bytes 786436
  43.1 26.3 %copy-start.3 = (bf16[4,2,512,256]{3,2,1,0:T(8,128)(2,1)S(1)}, bf16[4,2,512,256]{3,2,1,0:T(8,128)(2,1)}, u32[]{:S(2)}) copy-start(bf16[4,2,512,256]{3,2,1,0:T(8,128)(2,1)} %copy-done.2) | copy-start | bytes 6291460

commit v4 on v3

--- a/solution.py
+++ b/solution.py
@@ -37,16 +37,27 @@
     return jnp.where(position == order_of(row), 1.0, 0.0).astype(BF)
 
 
-def pack_kernel(coef_ref, ids_ref, send_ref, out_ref, all_ref, one_ref, extra_ref, sems):
+def pack_kernel(coef_ref, ids_ref, send_ref, out_ref, all_ref, one_ref, extra_ref, held_ref, sems):
     small = [pltpu.make_async_copy(ids_ref, all_ref, sems.at[0]), pltpu.make_async_copy(send_ref, one_ref, sems.at[1])]
+    width = MEMBERS * LANES // PIECES
+    fetched = [
+        pltpu.make_async_copy(
+            coef_ref.at[:, pl.ds(i * width, width)], held_ref.at[:, pl.ds(i * width, width)], sems.at[2 + 2 * MEMBERS + i]
+        )
+        for i in range(PIECES)
+    ]
     slices = [
         pltpu.make_async_copy(
-            coef_ref.at[:, pl.ds(t * LANES, LANES)], out_ref.at[t, pl.ds(0, CLUSTERS), :], sems.at[2 + t]
+            held_ref.at[:, pl.ds(t * LANES, LANES)], out_ref.at[t, pl.ds(0, CLUSTERS), :], sems.at[2 + t]
         )
         for t in range(MEMBERS)
     ]
-    for copy in small + slices:
+    for copy in small + fetched:
         copy.start()
+    for i in range(PIECES):
+        fetched[i].wait()
+        for copy in slices[i * (MEMBERS // PIECES) : (i + 1) * (MEMBERS // PIECES)]:
+            copy.start()
     sort = ordered_matrix()
     for copy in small:
         copy.wait()
@@ -224,7 +235,8 @@
 
         def write(m, value, turned, l=l):
             s_ref[l % 2, m] = value
-            t_ref[l % 2, m] = turned
+            if l < 3:
+                t_ref[l % 2, m] = turned
 
         level(read, read_turned, write, perm_ref[l], w_ref.at[l], kb_ref, mask)
     lane = lax.broadcasted_iota(jnp.int32, (LANES, LANES), 1).astype(F32)
@@ -299,6 +311,8 @@
 LIMIT = 24 * 1024 * 1024
 TABLES = 16 * 1024 * 1024
 SMALL = 4 * 1024 * 1024
+LARGE = 60 * 1024 * 1024
+PIECES = 4
 
 
 def call(kernel, name, out_shape, in_specs, scratch=(), out_spec=None, limit=None, flops=0, count=0):
@@ -333,10 +347,11 @@
             pltpu.VMEM((9, 1, CLUSTERS), jnp.int32),
             pltpu.VMEM((1, CLUSTERS), jnp.int32),
             pltpu.VMEM((EXTRA, LANES), BF),
-            pltpu.SemaphoreType.DMA((2 + 2 * MEMBERS,)),
+            pltpu.VMEM((CLUSTERS, MEMBERS * LANES), BF),
+            pltpu.SemaphoreType.DMA((2 + 2 * MEMBERS + PIECES,)),
         ),
         out_spec=HBM,
-        limit=SMALL,
+        limit=LARGE,
         count=2**21,
     )(coefficients[0, 0], lax.transpose(block_ids, (0, 3, 1, 2))[0], owner_order[0])
     x = lax.all_to_all(x, AXES, split_axis=0, concat_axis=0, tiled=True, axis_index_groups=SRC_GROUPS)

time: 107 us -> 106 us (level)
  local copies, waits for them, and re-layouts: 10.5 us -> 7.89 us
    unnamed x30 -> x24, local copies, waits for them, and re-layouts: 10.5 us -> 7.89 us
    pallas_call x1, Pallas kernels: 1.4 us -> 2.48 us  [on_device(): call(pack_kernel, 'pack', shape(MEMBERS, CLUSTERS + EXTRA, LANES), [HBM]...]
where the time goes in v4:
time: 106 us; the launch traced here: 105 us
  blocking collectives  48.3 us (46%)
  Pallas kernels  37.3 us (35%)
  local copies, waits for them, and re-layouts  7.89 us (7%)
  starting transfers between devices  6.93 us (7%)
  waiting for transfers between devices  4.47 us (4%)
    all_to_all x1, blocking collectives, on_device(): lax.all_to_all(mid, AXES, split_axis=0, concat_axis=0, tiled=True, axis_i...  26.3 us
    all_to_all x1, blocking collectives, on_device(): lax.all_to_all(done, AXES, split_axis=0, concat_axis=0, tiled=True, axis_...  22 us
    pallas_call x1, Pallas kernels, on_device(): call(observation_kernel, 'observation_levels', shape(MEMBERS, CLUSTERS, L...  14 us
    pallas_call x1, Pallas kernels, on_device(): call(source_kernel, 'source_levels', shape(NA, (MEMBERS + 1) * EXTRA, LAN...  13.8 us
    unnamed x24, local copies, waits for them, and re-layouts  7.89 us
    all_to_all x1, starting transfers between devices, on_device(): lax.all_to_all(x, AXES, split_axis=0, concat_axis=0, tiled=True, axis_ind...  6.93 us
    pallas_call x1, Pallas kernels, on_device(): call(table_kernel, 'tables', (shape(4, *square), shape(5, *square), shape...  5.88 us
    all_to_all x1, waiting for transfers between devices, on_device(): lax.all_to_all(x, AXES, split_axis=0, concat_axis=0, tiled=True, axis_ind...  4.47 us
  transfers between devices with their start and end apart: 1, of which 1 were waited for; matrix products, arithmetic and copies ran while one was open for 0% of the time, Pallas kernels for 6%

profile of v4, /device:TPU:1, one launch (start us, length us, event | category | flops | bytes accessed | tf_op | source)
XLA Modules:
  0.0 105.1 jit_solution(2444404936017374417)
XLA Ops:
  0.0 0.0 copy-start.8
  0.0 0.0 copy-start.11
  0.0 2.5 %pack.1 = bf16[16,288,128]{2,1,0:T(8,128)(2,1)} custom-call(bf16[256,2048]{1,0:T(8,128)(2,1)} %bitcast.8, s32[9,1,256]{2,1,0:T(1,128)} %bitcast.9, s32[1,256]{1,0:T(1,128)} %bitcast.10), custom_call_target="tpu_custom_call" | custom-call | bytes 2097152 | tf_op jit(solution)/shard_map/pack/pallas_call | solution.py:341
  2.5 6.9 %all-to-all-start = ((bf16[16,288,128]{2,1,0:T(8,128)(2,1)}), bf16[16,288,128]{2,1,0:T(8,128)(2,1)S(1)}, u32[]{:S(2)}, u32[]{:S(2)}) async-start(bf16[16,288,128]{2,1,0:T(8,128)(2,1)} %pack.1), calls=%async_computation | async-start | bytes 2359296 | tf_op jit(solution)/shard_map/all_to_all | solution.py:357
  9.4 0.0 copy-done.8
  9.4 0.0 copy-done.11
  9.4 0.0 copy-start
  9.5 1.6 %copy-done = bf16[4,16,2,2,32,32]{5,4,3,2,1,0:T(8,128)(2,1)S(1)} copy-done((bf16[4,16,2,2,32,32]{5,4,3,2,1,0:T(8,128)(2,1)S(1)}, bf16[4,16,2,2,32,32]{5,4,3,2,1,0:T(8,128)(2,1)}, u32[]{:S(2)}) %copy-start) | copy-done | bytes 524312
  11.0 0.0 copy-start.1
  11.0 1.6 %copy-done.1 = bf16[4,16,2,2,32,32]{5,4,3,2,1,0:T(8,128)(2,1)S(1)} copy-done((bf16[4,16,2,2,32,32]{5,4,3,2,1,0:T(8,128)(2,1)S(1)}, bf16[4,16,2,2,32,32]{5,4,3,2,1,0:T(8,128)(2,1)}, u32[]{:S(2)}) %copy-start.1) | copy-done | bytes 524312
  12.6 5.9 %tables.1 = (bf16[4,256,256]{2,1,0:T(8,128)(2,1)S(1)}, bf16[5,256,256]{2,1,0:T(8,128)(2,1)S(1)}, bf16[4,2,512,256]{3,2,1,0:T(8,128)(2,1)S(1)}, bf16[4,2,512,256]...) custom-call(bf16[4,16,2,2,32,32]{5,4,3,2,1,0:T(8,128)(2,1)S(1)} %copy-done, bf16[16,2,32,32]{3,2,1,0:T(8,128)(2,1)S(1)} %copy-done.8, ...), custom_call_target="tpu_custom_call" | custom-call | flops 1000000000 | bytes 16777216 | tf_op jit(solution)/shard_map/tables/pallas_call | solution.py:359
  18.5 0.0 copy-start.2
  18.5 1.3 %copy-done.2 = bf16[4,2,512,256]{3,2,1,0:T(8,128)(2,1)} copy-done((bf16[4,2,512,256]{3,2,1,0:T(8,128)(2,1)}, bf16[4,2,512,256]{3,2,1,0:T(8,128)(2,1)S(1)}, u32[]{:S(2)}) %copy-start.2) | copy-done | bytes 2097176
  19.8 0.0 copy-start.4
  19.9 0.8 copy-done.4
  20.7 0.0 copy-start.6
  20.7 0.8 copy-done.6
  21.5 0.0 copy-start.9
  21.5 0.7 copy-done.9
  22.2 0.1 pad_add_fusion.place_ref
  22.2 4.5 %all-to-all-done.x_ref = bf16[16,288,128]{2,1,0:T(8,128)(2,1)S(1)} async-done(((bf16[16,288,128]{2,1,0:T(8,128)(2,1)}), bf16[16,288,128]{2,1,0:T(8,128)(2,1)S(1)}, u32[]{:S(2)}, u32[]{:S(2)}) %all-to-all-start) | async-done | bytes 1179680 | tf_op jit(solution)/shard_map/all_to_all | solution.py:357
  26.7 0.0 copy-start.7
  26.7 1.0 copy-done.7
  27.8 0.0 copy-start.5
  27.8 0.0 copy-start.10
  27.8 13.8 %source_levels.1 = bf16[8,544,128]{2,1,0:T(8,128)(2,1)S(1)} custom-call(s32[2]{0:T(128)S(1)} %pad_add_fusion.place_ref, bf16[16,288,128]{2,1,0:T(8,128)(2,1)S(1)} %all-to-all-done.x_ref, bf16[4,256,256]{2,1,0:T(8,128)(2,1)S(1)} %copy-done.7, bf16[4,2,512,256]{3,2,1,0:T(8,128)(2,1)S(1)} %get-tuple-element.11.w_ref), custom_call_target="tpu_custom_call" | custom-call | tf_op jit(solution)/shard_map/source_levels/pallas_call | solution.py:372
  41.6 0.0 copy-start.3
  41.6 26.3 %all_to_all.15.r_ref = bf16[8,544,128]{2,1,0:T(8,128)(2,1)S(1)} all-to-all(bf16[8,544,128]{2,1,0:T(8,128)(2,1)S(1)} %source_levels.1), channel_id=1, replica_groups={{0,18,36,54,72,90,108,126},{1,19,37,55,73,91,109,127},{2,16,38,52,74,88..., dimensions={0} | all-to-all | bytes 2228224 | tf_op jit(solution)/shard_map/all_to_all | solution.py:379
  67.9 0.0 copy-done.5
  67.9 0.0 copy-done.10
  67.9 0.0 copy-done.3
  67.9 14.0 %observation_levels.1 = bf16[16,256,128]{2,1,0:T(8,128)(2,1)S(1)} custom-call(s32[2]{0:T(128)S(1)} %pad_add_fusion.place_ref, bf16[8,544,128]{2,1,0:T(8,128)(2,1)S(1)} %all_to_all.15.r_ref, bf16[5,256,256]{2,1,0:T(8,128)(2,1)S(1)} %copy-done.5, bf16[4,2,512,256]{3,2,1,0:T(8,128)(2,1)S(1)} %copy-done.3, bf16[2,256,256]{2,1,0:T(8,128)(2,1)S(1)} %copy-done.10), custom_call_target="tpu_custom_call" | custom-call | tf_op jit(solution)/shard_map/observation_levels/pallas_call | solution.py:380
  81.9 22.0 %all_to_all.16.x_ref = bf16[16,256,128]{2,1,0:T(8,128)(2,1)S(1)} all-to-all(bf16[16,256,128]{2,1,0:T(8,128)(2,1)S(1)} %observation_levels.1), channel_id=1, replica_groups={{0,1,2,3,4,5,6,7,8,9,10,11,12,13,14,15},{18,19,16,17,22,23,20,21,26,27,..., dimensions={0} | all-to-all | bytes 2097152 | tf_op jit(solution)/shard_map/all_to_all | solution.py:387
  103.9 1.1 %unpack.1 = bf16[256,2048]{1,0:T(8,128)(2,1)} custom-call(bf16[16,256,128]{2,1,0:T(8,128)(2,1)S(1)} %all_to_all.16.x_ref), custom_call_target="tpu_custom_call" | custom-call | bytes 2097152 | tf_op jit(solution)/shard_map/unpack/pallas_call | solution.py:388
Async XLA Ops:
  0.0 9.4 %copy-start.8 = (bf16[16,2,32,32]{3,2,1,0:T(8,128)(2,1)S(1)}, bf16[16,2,32,32]{3,2,1,0:T(8,128)(2,1)}, u32[]{:S(2)}) copy-start(bf16[16,2,32,32]{3,2,1,0:T(8,128)(2,1)} %mid_ref.1) | copy-start | bytes 196612
  0.0 9.4 %copy-start.11 = (s32[8,256]{1,0:T(8,128)S(1)}, s32[8,256]{1,0:T(8,128)}, u32[]{:S(2)}) copy-start(s32[8,256]{1,0:T(8,128)} %perm_ref.1) | copy-start | bytes 24580
  2.5 24.2 %all-to-all-start = ((bf16[16,288,128]{2,1,0:T(8,128)(2,1)}), bf16[16,288,128]{2,1,0:T(8,128)(2,1)S(1)}, u32[]{:S(2)}, u32[]{:S(2)}) async-start(bf16[16,288,128]{2,1,0:T(8,128)(2,1)} %pack.1), calls=%async_computation | async-start | bytes 2359296 | tf_op jit(solution)/shard_map/all_to_all | solution.py:357
  9.4 1.6 %copy-start = (bf16[4,16,2,2,32,32]{5,4,3,2,1,0:T(8,128)(2,1)S(1)}, bf16[4,16,2,2,32,32]{5,4,3,2,1,0:T(8,128)(2,1)}, u32[]{:S(2)}) copy-start(bf16[4,16,2,2,32,32]{5,4,3,2,1,0:T(8,128)(2,1)} %src_ref.1) | copy-start | bytes 1572868
  11.0 1.6 %copy-start.1 = (bf16[4,16,2,2,32,32]{5,4,3,2,1,0:T(8,128)(2,1)S(1)}, bf16[4,16,2,2,32,32]{5,4,3,2,1,0:T(8,128)(2,1)}, u32[]{:S(2)}) copy-start(bf16[4,16,2,2,32,32]{5,4,3,2,1,0:T(8,128)(2,1)} %obs_ref.1) | copy-start | bytes 1572868
  18.5 1.3 %copy-start.2 = (bf16[4,2,512,256]{3,2,1,0:T(8,128)(2,1)}, bf16[4,2,512,256]{3,2,1,0:T(8,128)(2,1)S(1)}, u32[]{:S(2)}) copy-start(bf16[4,2,512,256]{3,2,1,0:T(8,128)(2,1)S(1)} %get-tuple-element.13.w_ref) | copy-start | bytes 6291460
  19.8 0.8 copy-start.4
  20.7 0.8 copy-start.6
  21.5 0.7 copy-start.9
  26.7 1.0 copy-start.7
  27.8 40.1 %copy-start.5 = (bf16[5,256,256]{2,1,0:T(8,128)(2,1)S(1)}, bf16[5,256,256]{2,1,0:T(8,128)(2,1)}, u32[]{:S(2)}) copy-start(bf16[5,256,256]{2,1,0:T(8,128)(2,1)} %copy-done.4) | copy-start | bytes 1966084
  27.8 40.1 %copy-start.10 = (bf16[2,256,256]{2,1,0:T(8,128)(2,1)S(1)}, bf16[2,256,256]{2,1,0:T(8,128)(2,1)}, u32[]{:S(2)}) copy-start(bf16[2,256,256]{2,1,0:T(8,128)(2,1)} %copy-done.9) | copy-start | bytes 786436
  41.6 26.3 %copy-start.3 = (bf16[4,2,512,256]{3,2,1,0:T(8,128)(2,1)S(1)}, bf16[4,2,512,256]{3,2,1,0:T(8,128)(2,1)}, u32[]{:S(2)}) copy-start(bf16[4,2,512,256]{3,2,1,0:T(8,128)(2,1)} %copy-done.2) | copy-start | bytes 6291460

commit v5 on v4

--- a/solution.py
+++ b/solution.py
@@ -219,13 +219,17 @@
     lax.fori_loop(0, MEMBERS // BATCH, body, 0)
 
 
-def source_kernel(place_ref, x_ref, perm_ref, w_ref, out_ref, kt_ref, kb_ref, s_ref, t_ref, f_ref):
+def source_kernel(place_ref, x_ref, far_ref, w_ref, out_ref, kt_ref, kb_ref, s_ref, t_ref, f_ref, perm_ref, sem):
+    fetch = pltpu.make_async_copy(far_ref, perm_ref, sem)
+    fetch.start()
     b = place_ref[0]
     ids = x_ref[:, CLUSTERS : CLUSTERS + IDS, :].reshape(MEMBERS * IDS, LANES).astype(F32).T
     kt_ref[0] = ids
     kt_ref[1] = coded(ids)
     for l, mask in enumerate((2, 4, 8, 1)):
         spread_kinds(kt_ref.at[1], kb_ref, l)
+        if l == 0:
+            fetch.wait()
 
         def read(m, l=l):
             return x_ref[m, :CLUSTERS, :] if l == 0 else s_ref[(l - 1) % 2, m]
@@ -373,8 +377,11 @@
         source_kernel,
         "source_levels",
         shape(NA, (MEMBERS + 1) * EXTRA, LANES),
-        [SMEM, VMEM, VMEM, VMEM],
-        (ids, kinds, state, state, pltpu.VMEM((MEMBERS * CLUSTERS, LANES), F32)),
+        [SMEM, VMEM, HBM, VMEM],
+        (
+            ids, kinds, state, state, pltpu.VMEM((MEMBERS * CLUSTERS, LANES), F32),
+            pltpu.VMEM((4, *square), BF), pltpu.SemaphoreType.DMA(()),
+        ),
     )(place, x, src_perm, src_w)
     mid = lax.all_to_all(mid, AXES, split_axis=0, concat_axis=0, tiled=True, axis_index_groups=MID_GROUPS)
     done = call(

time: 106 us -> 107 us (level)
  Pallas kernels: 37.3 us -> 38.4 us
where the time goes in v5:
time: 107 us; the launch traced here: 106 us
  blocking collectives  48.3 us (45%)
  Pallas kernels  38.4 us (36%)
  local copies, waits for them, and re-layouts  7.89 us (7%)
  starting transfers between devices  6.93 us (6%)
  waiting for transfers between devices  4.47 us (4%)
    all_to_all x1, blocking collectives, on_device(): lax.all_to_all(mid, AXES, split_axis=0, concat_axis=0, tiled=True, axis_i...  26.3 us
    all_to_all x1, blocking collectives, on_device(): lax.all_to_all(done, AXES, split_axis=0, concat_axis=0, tiled=True, axis_...  22 us
    pallas_call x1, Pallas kernels, on_device(): call(source_kernel, 'source_levels', shape(NA, (MEMBERS + 1) * EXTRA, LAN...  14.9 us
    pallas_call x1, Pallas kernels, on_device(): call(observation_kernel, 'observation_levels', shape(MEMBERS, CLUSTERS, L...  14 us
    unnamed x24, local copies, waits for them, and re-layouts  7.89 us
    all_to_all x1, starting transfers between devices, on_device(): lax.all_to_all(x, AXES, split_axis=0, concat_axis=0, tiled=True, axis_ind...  6.93 us
    pallas_call x1, Pallas kernels, on_device(): call(table_kernel, 'tables', (shape(4, *square), shape(5, *square), shape...  5.88 us
    all_to_all x1, waiting for transfers between devices, on_device(): lax.all_to_all(x, AXES, split_axis=0, concat_axis=0, tiled=True, axis_ind...  4.47 us
  transfers between devices with their start and end apart: 1, of which 1 were waited for; matrix products, arithmetic and copies ran while one was open for 0% of the time, Pallas kernels for 6%

profile of v5, /device:TPU:1, one launch (start us, length us, event | category | flops | bytes accessed | tf_op | source)
XLA Modules:
  0.0 106.2 jit_solution(11847379729543657351)
XLA Ops:
  0.0 0.0 copy-start.8
  0.0 0.0 copy-start.11
  0.0 2.5 %pack.1 = bf16[16,288,128]{2,1,0:T(8,128)(2,1)} custom-call(bf16[256,2048]{1,0:T(8,128)(2,1)} %bitcast.8, s32[9,1,256]{2,1,0:T(1,128)} %bitcast.9, s32[1,256]{1,0:T(1,128)} %bitcast.10), custom_call_target="tpu_custom_call" | custom-call | bytes 2097152 | tf_op jit(solution)/shard_map/pack/pallas_call | solution.py:345
  2.5 6.9 %all-to-all-start = ((bf16[16,288,128]{2,1,0:T(8,128)(2,1)}), bf16[16,288,128]{2,1,0:T(8,128)(2,1)S(1)}, u32[]{:S(2)}, u32[]{:S(2)}) async-start(bf16[16,288,128]{2,1,0:T(8,128)(2,1)} %pack.1), calls=%async_computation | async-start | bytes 2359296 | tf_op jit(solution)/shard_map/all_to_all | solution.py:361
  9.4 0.0 copy-done.8
  9.4 0.0 copy-done.11
  9.4 0.0 copy-start
  9.5 1.6 %copy-done = bf16[4,16,2,2,32,32]{5,4,3,2,1,0:T(8,128)(2,1)S(1)} copy-done((bf16[4,16,2,2,32,32]{5,4,3,2,1,0:T(8,128)(2,1)S(1)}, bf16[4,16,2,2,32,32]{5,4,3,2,1,0:T(8,128)(2,1)}, u32[]{:S(2)}) %copy-start) | copy-done | bytes 524312
  11.0 0.0 copy-start.1
  11.0 1.6 %copy-done.1 = bf16[4,16,2,2,32,32]{5,4,3,2,1,0:T(8,128)(2,1)S(1)} copy-done((bf16[4,16,2,2,32,32]{5,4,3,2,1,0:T(8,128)(2,1)S(1)}, bf16[4,16,2,2,32,32]{5,4,3,2,1,0:T(8,128)(2,1)}, u32[]{:S(2)}) %copy-start.1) | copy-done | bytes 524312
  12.6 5.9 %tables.1 = (bf16[4,256,256]{2,1,0:T(8,128)(2,1)S(1)}, bf16[5,256,256]{2,1,0:T(8,128)(2,1)S(1)}, bf16[4,2,512,256]{3,2,1,0:T(8,128)(2,1)S(1)}, bf16[4,2,512,256]...) custom-call(bf16[4,16,2,2,32,32]{5,4,3,2,1,0:T(8,128)(2,1)S(1)} %copy-done, bf16[16,2,32,32]{3,2,1,0:T(8,128)(2,1)S(1)} %copy-done.8, ...), custom_call_target="tpu_custom_call" | custom-call | flops 1000000000 | bytes 16777216 | tf_op jit(solution)/shard_map/tables/pallas_call | solution.py:363
  18.5 0.0 copy-start.2
  18.5 1.3 %copy-done.2 = bf16[4,2,512,256]{3,2,1,0:T(8,128)(2,1)} copy-done((bf16[4,2,512,256]{3,2,1,0:T(8,128)(2,1)}, bf16[4,2,512,256]{3,2,1,0:T(8,128)(2,1)S(1)}, u32[]{:S(2)}) %copy-start.2) | copy-done | bytes 2097176
  19.8 0.0 copy-start.4
  19.9 0.8 copy-done.4
  20.7 0.0 copy-start.6
  20.7 0.8 copy-done.6
  21.5 0.0 copy-start.9
  21.5 0.7 copy-done.9
  22.2 0.1 pad_add_fusion.place_ref
  22.2 4.5 %all-to-all-done.x_ref = bf16[16,288,128]{2,1,0:T(8,128)(2,1)S(1)} async-done(((bf16[16,288,128]{2,1,0:T(8,128)(2,1)}), bf16[16,288,128]{2,1,0:T(8,128)(2,1)S(1)}, u32[]{:S(2)}, u32[]{:S(2)}) %all-to-all-start) | async-done | bytes 1179680 | tf_op jit(solution)/shard_map/all_to_all | solution.py:361
  26.7 0.0 copy-start.7
  26.7 1.0 copy-done.7
  27.8 0.0 copy-start.5
  27.8 0.0 copy-start.10
  27.8 14.9 %source_levels.1 = bf16[8,544,128]{2,1,0:T(8,128)(2,1)S(1)} custom-call(s32[2]{0:T(128)S(1)} %pad_add_fusion.place_ref, bf16[16,288,128]{2,1,0:T(8,128)(2,1)S(1)} %all-to-all-done.x_ref, bf16[4,256,256]{2,1,0:T(8,128)(2,1)S(1)} %copy-done.7, bf16[4,2,512,256]{3,2,1,0:T(8,128)(2,1)S(1)} %get-tuple-element.11.w_ref), custom_call_target="tpu_custom_call" | custom-call | tf_op jit(solution)/shard_map/source_levels/pallas_call | solution.py:376
  42.7 0.0 copy-start.3
  42.7 26.3 %all_to_all.15.r_ref = bf16[8,544,128]{2,1,0:T(8,128)(2,1)S(1)} all-to-all(bf16[8,544,128]{2,1,0:T(8,128)(2,1)S(1)} %source_levels.1), channel_id=1, replica_groups={{0,18,36,54,72,90,108,126},{1,19,37,55,73,91,109,127},{2,16,38,52,74,88..., dimensions={0} | all-to-all | bytes 2228224 | tf_op jit(solution)/shard_map/all_to_all | solution.py:386
  69.0 0.0 copy-done.5
  69.0 0.0 copy-done.10
  69.0 0.0 copy-done.3
  69.0 14.0 %observation_levels.1 = bf16[16,256,128]{2,1,0:T(8,128)(2,1)S(1)} custom-call(s32[2]{0:T(128)S(1)} %pad_add_fusion.place_ref, bf16[8,544,128]{2,1,0:T(8,128)(2,1)S(1)} %all_to_all.15.r_ref, bf16[5,256,256]{2,1,0:T(8,128)(2,1)S(1)} %copy-done.5, bf16[4,2,512,256]{3,2,1,0:T(8,128)(2,1)S(1)} %copy-done.3, bf16[2,256,256]{2,1,0:T(8,128)(2,1)S(1)} %copy-done.10), custom_call_target="tpu_custom_call" | custom-call | tf_op jit(solution)/shard_map/observation_levels/pallas_call | solution.py:387
  83.0 22.0 %all_to_all.16.x_ref = bf16[16,256,128]{2,1,0:T(8,128)(2,1)S(1)} all-to-all(bf16[16,256,128]{2,1,0:T(8,128)(2,1)S(1)} %observation_levels.1), channel_id=1, replica_groups={{0,1,2,3,4,5,6,7,8,9,10,11,12,13,14,15},{18,19,16,17,22,23,20,21,26,27,..., dimensions={0} | all-to-all | bytes 2097152 | tf_op jit(solution)/shard_map/all_to_all | solution.py:394
  105.0 1.1 %unpack.1 = bf16[256,2048]{1,0:T(8,128)(2,1)} custom-call(bf16[16,256,128]{2,1,0:T(8,128)(2,1)S(1)} %all_to_all.16.x_ref), custom_call_target="tpu_custom_call" | custom-call | bytes 2097152 | tf_op jit(solution)/shard_map/unpack/pallas_call | solution.py:395
Async XLA Ops:
  0.0 9.4 %copy-start.8 = (bf16[16,2,32,32]{3,2,1,0:T(8,128)(2,1)S(1)}, bf16[16,2,32,32]{3,2,1,0:T(8,128)(2,1)}, u32[]{:S(2)}) copy-start(bf16[16,2,32,32]{3,2,1,0:T(8,128)(2,1)} %mid_ref.1) | copy-start | bytes 196612
  0.0 9.4 %copy-start.11 = (s32[8,256]{1,0:T(8,128)S(1)}, s32[8,256]{1,0:T(8,128)}, u32[]{:S(2)}) copy-start(s32[8,256]{1,0:T(8,128)} %perm_ref.1) | copy-start | bytes 24580
  2.5 24.2 %all-to-all-start = ((bf16[16,288,128]{2,1,0:T(8,128)(2,1)}), bf16[16,288,128]{2,1,0:T(8,128)(2,1)S(1)}, u32[]{:S(2)}, u32[]{:S(2)}) async-start(bf16[16,288,128]{2,1,0:T(8,128)(2,1)} %pack.1), calls=%async_computation | async-start | bytes 2359296 | tf_op jit(solution)/shard_map/all_to_all | solution.py:361
  9.4 1.6 %copy-start = (bf16[4,16,2,2,32,32]{5,4,3,2,1,0:T(8,128)(2,1)S(1)}, bf16[4,16,2,2,32,32]{5,4,3,2,1,0:T(8,128)(2,1)}, u32[]{:S(2)}) copy-start(bf16[4,16,2,2,32,32]{5,4,3,2,1,0:T(8,128)(2,1)} %src_ref.1) | copy-start | bytes 1572868
  11.0 1.6 %copy-start.1 = (bf16[4,16,2,2,32,32]{5,4,3,2,1,0:T(8,128)(2,1)S(1)}, bf16[4,16,2,2,32,32]{5,4,3,2,1,0:T(8,128)(2,1)}, u32[]{:S(2)}) copy-start(bf16[4,16,2,2,32,32]{5,4,3,2,1,0:T(8,128)(2,1)} %obs_ref.1) | copy-start | bytes 1572868
  18.5 1.3 %copy-start.2 = (bf16[4,2,512,256]{3,2,1,0:T(8,128)(2,1)}, bf16[4,2,512,256]{3,2,1,0:T(8,128)(2,1)S(1)}, u32[]{:S(2)}) copy-start(bf16[4,2,512,256]{3,2,1,0:T(8,128)(2,1)S(1)} %get-tuple-element.13.w_ref) | copy-start | bytes 6291460
  19.8 0.8 copy-start.4
  20.7 0.8 copy-start.6
  21.5 0.7 copy-start.9
  26.7 1.0 copy-start.7
  27.8 41.2 %copy-start.5 = (bf16[5,256,256]{2,1,0:T(8,128)(2,1)S(1)}, bf16[5,256,256]{2,1,0:T(8,128)(2,1)}, u32[]{:S(2)}) copy-start(bf16[5,256,256]{2,1,0:T(8,128)(2,1)} %copy-done.4) | copy-start | bytes 1966084
  27.8 41.2 %copy-start.10 = (bf16[2,256,256]{2,1,0:T(8,128)(2,1)S(1)}, bf16[2,256,256]{2,1,0:T(8,128)(2,1)}, u32[]{:S(2)}) copy-start(bf16[2,256,256]{2,1,0:T(8,128)(2,1)} %copy-done.9) | copy-start | bytes 786436
  42.7 26.3 %copy-start.3 = (bf16[4,2,512,256]{3,2,1,0:T(8,128)(2,1)S(1)}, bf16[4,2,512,256]{3,2,1,0:T(8,128)(2,1)}, u32[]{:S(2)}) copy-start(bf16[4,2,512,256]{3,2,1,0:T(8,128)(2,1)} %copy-done.2) | copy-start | bytes 6291460
